TPU v7x, 768 devices: a whole 4x8x12 slice. The times are simulated.
768 devices in a mesh: dom: 96 (over y, z), sub: 8 (over x, core).
Axes of the slice: x: 4, y: 8, z: 12, core: 2. Of those that a mesh axis runs over, the one named last changes fastest.
Arguments:
- start: float32 [64, 196608], P(None, ('dom', 'sub'))
- links: int32 [20, 196608], P(None, ('dom', 'sub')), may hold values from 0 to 1791, as said below
- link_weight: float32 [20, 196608], P(None, ('dom', 'sub')), may hold values from 0 to 1, as said below
- pool_slot: int32 [196608], P(('dom', 'sub')), may hold values from -1 to 511, as said below
Outputs:
- eigen_block: float32 [64, 196608], P(None, ('dom', 'sub'))
- ritz_block: float32 [64, 64], replicated
Inputs may be any that keep to these rules, and one draw needn't show every extreme that they name: Entries below 256 name a node of the same device; entries from 256 on name a slot of the pool of the group before, the own group or the group after, 512 slots each, and only nodes with a pool slot have such links; links to a group outside the grid do not occur; an entry with zero weight is padding and names 0. `link_weight`: the affinity is symmetric: where node i links to node j with weight w, node j links to node i with weight w; every node has positive weight on its first 14 links; zero marks padding. `pool_slot`: within each partition group every slot 0 to 511 is held by exactly one node; the number of slots a device holds differs from device to device.
All inputs are finite; a program needn't handle non-finite values.
Results may differ from a plain program's by a relative error of at most 0.00005.
Values sent between devices are 32-bit elements; how exact they have to be, the bound alone decides.
A program may use at most 32 MiB of HBM per device.

v0:
```python
import jax
import jax.numpy as jnp
from jax import lax
from jax.sharding import PartitionSpec as P

SLOT_DEV = 64


def padded(cells, sides, width):
    for axis, dim in sides:
        count = lax.axis_size(axis)
        ends = count - 1
        head = lax.slice_in_dim(cells, 0, width, axis=dim)
        tail = lax.slice_in_dim(cells, cells.shape[dim] - width, cells.shape[dim], axis=dim)
        cells = jnp.concatenate(
            [
                lax.ppermute(tail, axis, [(i, (i + 1) % count) for i in range(ends)]),
                cells,
                lax.ppermute(head, axis, [((i + 1) % count, i) for i in range(ends)]),
            ],
            axis=dim,
        )
    return cells


def products(left_side, right_side):
    return jnp.dot(left_side, right_side.T, precision=lax.Precision.HIGHEST)


def reduce_basis(gram_sum, mixed_sum, block_size):
    highest = lax.Precision.HIGHEST
    basis_size = gram_sum.shape[0]
    lower_fac = jnp.linalg.cholesky(gram_sum)
    symmetric = 0.5 * (mixed_sum + mixed_sum.T)
    halfway = lax.linalg.triangular_solve(lower_fac, symmetric, left_side=True, lower=True)
    reduced = lax.linalg.triangular_solve(lower_fac, halfway.T, left_side=True, lower=True)
    shifted = 0.5 * (reduced + jnp.eye(basis_size, dtype=jnp.float32))
    filtered = jnp.dot(shifted, shifted, precision=highest)
    filtered = jnp.dot(filtered, filtered, precision=highest)
    start_coords = lower_fac.T[:, :block_size]
    tilted = jnp.dot(filtered, start_coords, precision=highest)
    factor = jnp.linalg.cholesky(jnp.dot(tilted.T, tilted, precision=highest))
    orthonormal = lax.linalg.triangular_solve(factor, tilted.T, left_side=True, lower=True).T
    coeffs = lax.linalg.triangular_solve(
        lower_fac, orthonormal, left_side=True, lower=True, transpose_a=True
    )
    ritz_part = jnp.dot(
        orthonormal.T, jnp.dot(reduced, orthonormal, precision=highest), precision=highest
    )
    return (coeffs, ritz_part)


def per_device(start, links, link_weight, pool_slot):
    highest = lax.Precision.HIGHEST
    block_size = start.shape[0]
    row_count = start.shape[1]
    link_count = links.shape[0]
    node_count = row_count * lax.axis_size("dom") * lax.axis_size("sub")
    slot_count = SLOT_DEV * lax.axis_size("sub")
    degree = jnp.sum(link_weight, axis=0)
    root = lax.rsqrt(degree)
    target = jnp.where(pool_slot >= 0, pool_slot, slot_count)
    flat_links = links.reshape(-1)

    def affinity(vectors):
        scaled = root * vectors
        placed = (
            jnp.zeros((block_size, slot_count + 1), jnp.float32)
            .at[:, target]
            .add(scaled)[:, :slot_count]
        )
        pooled = lax.psum(placed, "sub")
        beside_all = padded(pooled[None], (("dom", 0),), 1)
        lookup = jnp.concatenate([scaled, beside_all[0], beside_all[1], beside_all[2]], axis=1)
        picked = jnp.take(lookup, flat_links, axis=1).reshape(block_size, link_count, row_count)
        summed = jnp.sum(picked * link_weight[None], axis=1)
        return root * summed

    def ritz_sums(basis, front, pending, back):
        images = affinity(pending)
        stacked = [front, images] if back is None else [front, images, back]
        gram_sum, mixed_sum = lax.psum(
            (products(basis, basis), products(basis, jnp.concatenate(stacked, axis=0))),
            ("dom", "sub"),
        )
        return (gram_sum / node_count, mixed_sum / node_count, images)

    image_x = affinity(start)
    basis_one = jnp.concatenate([start, image_x], axis=0)
    gram_one, mixed_one, image_w = ritz_sums(basis_one, image_x, image_x, None)
    coeffs_one, theta_one = reduce_basis(gram_one, mixed_one, block_size)
    images_one = jnp.concatenate([image_x, image_w], axis=0)
    current = jnp.dot(coeffs_one.T, basis_one, precision=highest)
    current_img = jnp.dot(coeffs_one.T, images_one, precision=highest)
    tail_coef = coeffs_one[block_size:]
    search = jnp.dot(tail_coef.T, image_x, precision=highest)
    search_img = jnp.dot(tail_coef.T, image_w, precision=highest)
    residual = current_img - jnp.dot(theta_one.T, current, precision=highest)
    basis_two = jnp.concatenate([current, residual, search], axis=0)
    gram_two, mixed_two, residual_img = ritz_sums(basis_two, current_img, residual, search_img)
    coeffs_two, ritz_block = reduce_basis(gram_two, mixed_two, block_size)
    eigen_block = jnp.dot(coeffs_two.T, basis_two, precision=highest)
    return (eigen_block, ritz_block)


def solution(mesh):
    placed = (
        P(None, ("dom", "sub")),
        P(None, ("dom", "sub")),
        P(None, ("dom", "sub")),
        P(("dom", "sub")),
    )
    return jax.shard_map(
        per_device,
        mesh=mesh,
        in_specs=placed,
        out_specs=(P(None, ("dom", "sub")), P()),
        check_vma=False,
    )
```

profile of v0, /device:TPU:1, one launch (start us, length us, event | category | flops | bytes accessed | tf_op | source)
XLA Modules:
  0.0 1404.3 jit_solution(16293349373771961878)
XLA Ops:
  9.6 1.8 scatter_custom_fusion
  14.5 81.2 %all-reduce.13.cloned.1.call-done = f32[64,512]{0,1:T(8,128)} async-done(((f32[64,512]{0,1:T(8,128)}), f32[64,512]{0,1:T(8,128)}) %all-reduce.13.cloned.1.call-update) | async-done | bytes 131088 | tf_op jit(solution)/shard_map/psum | solution.py:72
  95.7 1.3 collective-permute-start.1
  97.0 4.0 collective-permute-start
  101.0 3.2 collective-permute-done.1
  106.3 15.9 %gather_fusion = f32[5120,64]{1,0:T(8,128)S(1)} fusion(f32[64,1792]{0,1:T(8,128)S(1)} %pad_maximum_fusion, s32[5120]{0:T(1024)} %fusion.79), kind=kCustom, calls=%fused_computation.clone | custom fusion | bytes 2641920 | tf_op jit(solution)/shard_map/jit(_take)/gather | solution.py:75
  122.1 2.7 broadcast_select_fusion.2
  125.9 1.8 scatter_custom_fusion.1
  128.5 79.6 %all-reduce.15.cloned.1.call-done = f32[64,512]{0,1:T(8,128)} async-done(((f32[64,512]{0,1:T(8,128)}), f32[64,512]{0,1:T(8,128)}) %all-reduce.15.cloned.1.call-update) | async-done | bytes 131088 | tf_op jit(solution)/shard_map/psum | solution.py:72
  208.2 1.3 collective-permute-start.3
  209.4 4.0 collective-permute-start.2
  214.5 2.2 collective-permute-done.3
  218.7 15.9 %gather_fusion.1 = f32[5120,64]{1,0:T(8,128)S(1)} fusion(f32[64,1792]{0,1:T(8,128)S(1)} %pad_maximum_fusion.1, s32[5120]{0:T(1024)} %fusion.79), kind=kCustom, calls=%fused_computation.1.clone | custom fusion | bytes 2641920 | tf_op jit(solution)/shard_map/jit(_take)/gather | solution.py:75
  234.6 2.7 broadcast_select_fusion.1
  239.4 466.9 %all-reduce.21.cloned.1.call-done = (f32[128,128]{0,1:T(8,128)}, f32[128,128]{0,1:T(8,128)}) async-done(((f32[128,128]{0,1:T(8,128)}, f32[128,128]{0,1:T(8,128)}), (f32[128,128]{0,1:T(8,128)}, f32[128,128]{0,1:T(8,128)})) %all-reduce.21.cloned.1.call-update) | async-done | bytes 131088 | tf_op jit(solution)/shard_map/psum | solution.py:82
  708.4 11.7 cholesky.98
  721.4 9.8 custom-call.34
  733.6 5.8 cholesky.205
  740.8 4.9 custom-call.35
  747.5 1.8 scatter_custom_fusion.2
  750.9 70.3 %all-reduce.17.cloned.1.call-done = f32[64,512]{0,1:T(8,128)} async-done(((f32[64,512]{0,1:T(8,128)}), f32[64,512]{0,1:T(8,128)}) %all-reduce.17.cloned.1.call-update) | async-done | bytes 131088 | tf_op jit(solution)/shard_map/psum | solution.py:72
  822.5 4.0 collective-permute-start.4
  827.9 1.8 collective-permute-done.5
  831.8 16.1 %gather_fusion.2 = f32[5120,64]{1,0:T(8,128)S(1)} fusion(f32[64,1792]{0,1:T(8,128)S(1)} %pad_maximum_fusion.2, s32[5120]{0:T(1024)} %fusion.79), kind=kCustom, calls=%fused_computation.2.clone | custom fusion | bytes 2641920 | tf_op jit(solution)/shard_map/jit(_take)/gather | solution.py:75
  847.9 2.7 broadcast_select_fusion
  852.7 473.5 %all-reduce.19.cloned.1.call-done = (f32[192,192]{0,1:T(8,128)}, f32[192,192]{0,1:T(8,128)}) async-done(((f32[192,192]{0,1:T(8,128)}, f32[192,192]{0,1:T(8,128)}), (f32[192,192]{0,1:T(8,128)}, f32[192,192]{0,1:T(8,128)})) %all-reduce.19.cloned.1.call-update) | async-done | bytes 294928 | tf_op jit(solution)/shard_map/psum | solution.py:82
  1328.4 11.7 cholesky.161
  1340.2 9.8 custom-call.36
  1350.4 5.8 cholesky.175
  1359.2 19.9 %custom-call.37 = f32[2,128,128]{1,2,0:T(8,128)S(1)} custom-call(f32[2,128,128]{2,1,0:T(8,128)S(1)} %pad_maximum_fusion.9), custom_call_target="InvertDiagBlocksLowerTriangular" | custom-call | tf_op jit(solution)/shard_map/triangular_solve | solution.py:44
  1382.6 5.8 cholesky.216
  1389.8 4.9 custom-call.38
  (157 shorter events, 43.4 us)
Async XLA Ops:
  7.2 88.6 %all-reduce.13.cloned.1.call-start = ((), (), s32[]{:S(2)}) async-start(), calls=%async_computation | async-start | bytes 524288 | tf_op jit(solution)/shard_map/psum | solution.py:72
  12.1 196.0 %all-reduce.15.cloned.1.call-start = ((), (), s32[]{:S(2)}) async-start(), calls=%async_computation.1 | async-start | bytes 524288 | tf_op jit(solution)/shard_map/psum | solution.py:72
  95.7 8.5 collective-permute-start.1
  97.0 8.2 collective-permute-start
  122.1 2.7 copy-start.13
  124.8 88.7 %copy-start.2 = (f32[64,256]{1,0:T(8,128)S(1)}, f32[64,256]{1,0:T(8,128)}, u32[]{:S(2)}) copy-start(f32[64,256]{1,0:T(8,128)} %param.11) | copy-start | bytes 196612
  125.8 91.9 %copy-start = (f32[64,256]{1,0:T(8,128)}, f32[64,256]{1,0:T(8,128)S(1)}, u32[]{:S(2)}) copy-start(f32[64,256]{1,0:T(8,128)S(1)} %get-tuple-element.57) | copy-start | bytes 196612
  128.5 577.9 %all-reduce.21.cloned.1.call-start = ((), (), s32[]{:S(2)}) async-start(), calls=%async_computation.4 | async-start | bytes 262144 | tf_op jit(solution)/shard_map/psum | solution.py:82
  208.2 8.5 collective-permute-start.3
  209.4 8.2 collective-permute-start.2
  234.6 2.7 copy-start.14
  237.3 1.0 copy-start.1
  237.3 1.0 copy-start.3
  239.2 582.0 %all-reduce.17.cloned.1.call-start = ((), (), s32[]{:S(2)}) async-start(), calls=%async_computation.2 | async-start | bytes 524288 | tf_op jit(solution)/shard_map/psum | solution.py:72
  746.6 0.7 copy-start.11
  746.9 83.9 %copy-start.4 = (f32[64,256]{1,0:T(8,128)}, f32[64,256]{1,0:T(8,128)S(1)}, u32[]{:S(2)}) copy-start(f32[64,256]{1,0:T(8,128)S(1)} %fusion.31) | copy-start | bytes 196612
  747.3 83.4 %copy-start.8 = (f32[64,256]{1,0:T(8,128)}, f32[64,256]{1,0:T(8,128)S(1)}, u32[]{:S(2)}) copy-start(f32[64,256]{1,0:T(8,128)S(1)} %get-tuple-element.67) | copy-start | bytes 196612
  750.0 576.2 %all-reduce.19.cloned.1.call-start = ((), (), s32[]{:S(2)}) async-start(), calls=%async_computation.3 | async-start | bytes 786432 | tf_op jit(solution)/shard_map/psum | solution.py:82
  821.2 8.5 collective-permute-start.5
  822.5 8.2 collective-permute-start.4
  826.8 4.0 copy-start.6
  847.8 2.8 copy-start.15
  850.5 1.0 copy-start.5
  850.6 1.0 copy-start.7
  850.6 1.0 copy-start.9
  850.6 1.0 copy-start.12
  850.6 1.0 copy-start.16
  1326.2 32.7 %copy-start.10 = (f32[192,192]{0,1:T(8,128)S(1)}, f32[192,192]{0,1:T(8,128)}, u32[]{:S(2)}) copy-start(f32[192,192]{0,1:T(8,128)} %get-tuple-element.52) | copy-start | bytes 442372
Sparse Core Ops, SparseCore 0:
  12.3 83.4 all-reduce.12
  128.6 79.5 all-reduce.14
  239.3 466.9 all-reduce.20
  750.1 71.0 all-reduce.16
  852.8 473.3 all-reduce.18
where the time goes:
time: 1410 us; the launch traced here: 1400 us
  waiting for transfers between devices  1180 us (84%)
  other arithmetic  122 us (9%)
  local copies, waits for them, and re-layouts  52.5 us (4%)
  starting transfers between devices  16.2 us (1%)
  between operations  16 us (1%)
  matrix products  15.3 us (1%)
    psum x2, waiting for transfers between devices, ritz_sums(): lax.psum((products(basis, basis), products(basis, jnp.concatenate(stacked...  940 us
    psum x3, waiting for transfers between devices, affinity(): pooled = lax.psum(placed, 'sub')  231 us
    gather x3, local copies, waits for them, and re-layouts, affinity(): jnp.take(lookup, flat_links, axis=1)  47.8 us
    another operation x10, other arithmetic, reduce_basis(): lower_fac = jnp.linalg.cholesky(gram_sum)  41.1 us
    another operation x6, other arithmetic, reduce_basis(): lax.linalg.triangular_solve(lower_fac, orthonormal, left_side=True, lower...  29.9 us
  transfers between devices with their start and end apart: 11, of which 11 were waited for; matrix products, arithmetic and copies ran while one was open for 0% of the time, Pallas kernels for 0%

commit v1 on v0

v1 whole, which is shorter than its diff:
```python
import functools

import jax
import jax.numpy as jnp
from jax import lax
from jax.experimental import pallas as pl
from jax.experimental.pallas import tpu as pltpu
from jax.sharding import PartitionSpec as P

MESH = pl.DeviceIdType.MESH
VMEM = pltpu.VMEM
DMA = pltpu.SemaphoreType.DMA
SLOT_DEV = 64
ROUNDS = 3
BUILD_ROWS = 64
N_Z = 12


def split(values):
    high = values.astype(jnp.bfloat16)
    low = (values - high.astype(jnp.float32)).astype(jnp.bfloat16)
    return high, low


def outer(left, right):
    return lax.dot_general(
        left,
        right,
        (((1,), (1,)), ((), ())),
        precision=lax.Precision.HIGHEST,
        preferred_element_type=jnp.float32,
    )


def each(low, high, body):
    lax.fori_loop(low, high, lambda k, c: (body(k), c)[1], 0)


def sums_kernel(
    n_dom,
    n_sub,
    start_ref,
    links_ref,
    weight_ref,
    slot_ref,
    one_ref,
    two_ref,
    sums_ref,
    root_ref,
    place_ref,
    table_hi,
    table_lo,
    contrib,
    gathered,
    pools,
    partial,
    part_in,
    z_in,
    y_in,
    rs_send,
    rs_recv,
    ag_send,
    ag_recv,
    part_send,
    part_recv,
    z_send,
    z_recv,
    y_send,
    y_recv,
    out_send,
    out_recv,
):
    dom = lax.axis_index("dom")
    sub = lax.axis_index("sub")
    n_y = n_dom // N_Z
    row = dom // N_Z
    col = dom % N_Z
    block = start_ref.shape[0]
    nodes = start_ref.shape[1]
    slots = place_ref.shape[0]
    share = block // n_sub
    part = partial.shape[0] // n_sub

    def sub_peer(k):
        return (sub + k) % n_sub

    def dom_peer(area):
        return (dom + area + n_dom - 1) % n_dom

    def z_peer(k):
        return (col + k) % N_Z

    def y_peer(k):
        return (row + k) % n_y

    def remote(src, dst, send, recv, d, s):
        return pltpu.make_async_remote_copy(
            src_ref=src, dst_ref=dst, send_sem=send, recv_sem=recv,
            device_id=(d, s), device_id_type=MESH,
        )

    barrier = pltpu.get_barrier_semaphore()

    def greet(d, s):
        pl.semaphore_signal(barrier, inc=1, device_id=(d, s), device_id_type=MESH)

    each(1, n_sub, lambda k: greet(dom, sub_peer(k)))
    each(0, n_sub, lambda k: greet(dom_peer(0), k))
    each(0, n_sub, lambda k: greet(dom_peer(2), k))
    each(1, N_Z, lambda k: greet(row * N_Z + z_peer(k), sub))
    each(1, n_y, lambda k: greet(y_peer(k) * N_Z + col, sub))

    def rs_copy(j, peer, at):
        return remote(contrib.at[j, peer], gathered.at[j, at],
                      rs_send.at[j, peer], rs_recv.at[j, at], dom, peer)

    def ag_copy(j, to, peer, area, at):
        return remote(pools.at[j, 1, sub], pools.at[j, area, at],
                      ag_send.at[j, to, peer], ag_recv.at[j, area, at], dom_peer(to), peer)

    def rows_of(p):
        return pl.ds(pl.multiple_of(p * part, part), part)

    def part_copy(peer, at):
        return remote(partial.at[rows_of(peer)], part_in.at[at],
                      part_send.at[peer], part_recv.at[at], dom, peer)

    def z_copy(peer, at):
        return remote(z_in.at[col], z_in.at[at],
                      z_send.at[peer], z_recv.at[at], row * N_Z + peer, sub)

    def y_copy(peer, at):
        return remote(y_in.at[row], y_in.at[at],
                      y_send.at[peer], y_recv.at[at], peer * N_Z + col, sub)

    def out_copy(peer, at):
        return remote(sums_ref.at[rows_of(sub)], sums_ref.at[rows_of(at)],
                      out_send.at[peer], out_recv.at[at], dom, peer)

    def total(ref, count):
        result = ref[0]
        for k in range(1, count):
            result = result + ref[k]
        return result

    root_ref[...] = lax.rsqrt(jnp.sum(weight_ref[...], axis=0, keepdims=True))

    def place(i, carry):
        base = pl.multiple_of(i * BUILD_ROWS, BUILD_ROWS)
        ids = base + lax.broadcasted_iota(jnp.int32, (BUILD_ROWS, nodes), 0)
        place_ref[pl.ds(base, BUILD_ROWS), :] = jnp.where(
            ids == slot_ref[...], 1.0, 0.0
        ).astype(jnp.bfloat16)
        return carry

    lax.fori_loop(0, slots // BUILD_ROWS, place, 0)

    def build(i, carry):
        base = pl.multiple_of(i * BUILD_ROWS, BUILD_ROWS)
        ids = base + lax.broadcasted_iota(jnp.int32, (BUILD_ROWS, nodes), 0)
        summed = jnp.zeros((BUILD_ROWS, nodes), jnp.float32)
        for k in range(links_ref.shape[0]):
            summed = summed + jnp.where(
                ids == links_ref[k : k + 1, :], weight_ref[k : k + 1, :], 0.0
            )
        high, low = split(summed * root_ref[...])
        table_hi[pl.ds(base, BUILD_ROWS), :] = high
        table_lo[pl.ds(base, BUILD_ROWS), :] = low
        return carry

    def contribute(j, vectors):
        high, low = split(root_ref[...] * vectors)
        spread = lax.dot_general(
            jnp.concatenate([high, low], axis=0),
            place_ref[...],
            (((1,), (1,)), ((), ())),
            preferred_element_type=jnp.float32,
        )
        contrib[j] = (spread[:block] + spread[block:]).reshape(n_sub, share, slots)
        return high, low

    def apply(high, low, first, count):
        upper = jnp.dot(
            jnp.concatenate([high, low], axis=0),
            table_hi[first : first + count, :],
            preferred_element_type=jnp.float32,
        )
        lower = jnp.dot(
            high, table_lo[first : first + count, :], preferred_element_type=jnp.float32
        )
        return upper[:block] + upper[block:] + lower

    def affinity(j, vectors, meanwhile):
        high, low = contribute(j, vectors)
        if j == 0:
            pl.semaphore_wait(barrier, 3 * n_sub - 1 + N_Z - 1 + n_y - 1)
        each(1, n_sub, lambda k: rs_copy(j, sub_peer(k), sub).start())
        if j == 0:
            lax.fori_loop(0, table_hi.shape[0] // BUILD_ROWS, build, 0)
        gathered[j, sub] = contrib[j, sub]
        summed = apply(high, low, 0, nodes)
        each(1, n_sub, lambda k: rs_copy(j, sub_peer(k), sub_peer(k)).wait_recv())
        pools[j, 1, sub] = total(gathered.at[j], n_sub)
        each(1, n_sub, lambda k: ag_copy(j, 1, sub_peer(k), 1, sub).start())
        each(0, n_sub, lambda k: ag_copy(j, 0, k, 2, sub).start())
        each(0, n_sub, lambda k: ag_copy(j, 2, k, 0, sub).start())
        meanwhile()
        each(1, n_sub, lambda k: ag_copy(j, 1, sub_peer(k), 1, sub_peer(k)).wait_recv())
        for area in (1, 0, 2):
            if area != 1:
                each(0, n_sub, lambda k: ag_copy(j, area, k, area, k).wait_recv())
            high, low = split(pools[j, area].reshape(block, slots))
            summed = summed + apply(high, low, nodes + area * slots, slots)
        return summed

    def moments_zero():
        partial[0:block, 0:block] = outer(start_ref[...], start_ref[...])

    def moments_one():
        partial[0:block, block : 2 * block] = outer(start_ref[...], one_ref[...])
        partial[block : 2 * block, 0:block] = outer(one_ref[...], one_ref[...])

    def moments_two():
        partial[block : 2 * block, block : 2 * block] = outer(one_ref[...], two_ref[...])
        partial[2 * block : 3 * block, 0:block] = outer(two_ref[...], two_ref[...])

    one_ref[...] = affinity(0, start_ref[...], moments_zero)
    two_ref[...] = affinity(1, one_ref[...], moments_one)
    three = affinity(2, two_ref[...], moments_two)
    partial[2 * block : 3 * block, block : 2 * block] = outer(two_ref[...], three)

    each(1, n_sub, lambda k: part_copy(sub_peer(k), sub).start())
    part_in[sub] = partial[rows_of(sub), :]
    each(1, n_sub, lambda k: part_copy(sub_peer(k), sub_peer(k)).wait_recv())
    z_in[col] = total(part_in, n_sub)
    each(1, N_Z, lambda k: z_copy(z_peer(k), col).start())
    each(1, N_Z, lambda k: z_copy(z_peer(k), z_peer(k)).wait_recv())
    y_in[row] = total(z_in, N_Z)
    each(1, n_y, lambda k: y_copy(y_peer(k), row).start())
    each(1, n_y, lambda k: y_copy(y_peer(k), y_peer(k)).wait_recv())
    sums_ref[rows_of(sub), :] = total(y_in, n_y)
    each(1, n_sub, lambda k: out_copy(sub_peer(k), sub).start())
    each(1, n_sub, lambda k: out_copy(sub_peer(k), sub_peer(k)).wait_recv())

    for j in range(ROUNDS):
        each(1, n_sub, lambda k: rs_copy(j, sub_peer(k), sub).wait_send())
        each(1, n_sub, lambda k: ag_copy(j, 1, sub_peer(k), 1, sub).wait_send())
        each(0, n_sub, lambda k: ag_copy(j, 0, k, 2, sub).wait_send())
        each(0, n_sub, lambda k: ag_copy(j, 2, k, 0, sub).wait_send())
    each(1, n_sub, lambda k: part_copy(sub_peer(k), sub).wait_send())
    each(1, N_Z, lambda k: z_copy(z_peer(k), col).wait_send())
    each(1, n_y, lambda k: y_copy(y_peer(k), row).wait_send())
    each(1, n_sub, lambda k: out_copy(sub_peer(k), sub).wait_send())


def powers_and_sums(start, links, link_weight, pool_slot):
    n_dom = lax.axis_size("dom")
    n_sub = lax.axis_size("sub")
    n_y = n_dom // N_Z
    block, nodes = start.shape
    slots = SLOT_DEV * n_sub
    share = block // n_sub
    part = 3 * block // n_sub
    entries = nodes + 3 * slots
    vectors = jax.ShapeDtypeStruct((block, nodes), jnp.float32)
    f32 = jnp.float32
    return pl.pallas_call(
        functools.partial(sums_kernel, n_dom, n_sub),
        out_shape=(vectors, vectors, jax.ShapeDtypeStruct((3 * block, 2 * block), f32)),
        in_specs=[pl.BlockSpec(memory_space=VMEM)] * 4,
        out_specs=(pl.BlockSpec(memory_space=VMEM),) * 3,
        scratch_shapes=[
            VMEM((1, nodes), f32),
            VMEM((slots, nodes), jnp.bfloat16),
            VMEM((entries, nodes), jnp.bfloat16),
            VMEM((entries, nodes), jnp.bfloat16),
            VMEM((ROUNDS, n_sub, share, slots), f32),
            VMEM((ROUNDS, n_sub, share, slots), f32),
            VMEM((ROUNDS, 3, n_sub, share, slots), f32),
            VMEM((3 * block, 2 * block), f32),
            VMEM((n_sub, part, 2 * block), f32),
            VMEM((N_Z, part, 2 * block), f32),
            VMEM((n_y, part, 2 * block), f32),
            DMA((ROUNDS, n_sub)),
            DMA((ROUNDS, n_sub)),
            DMA((ROUNDS, 3, n_sub)),
            DMA((ROUNDS, 3, n_sub)),
            DMA((n_sub,)),
            DMA((n_sub,)),
            DMA((N_Z,)),
            DMA((N_Z,)),
            DMA((n_y,)),
            DMA((n_y,)),
            DMA((n_sub,)),
            DMA((n_sub,)),
        ],
        compiler_params=pltpu.CompilerParams(
            collective_id=0, has_side_effects=True, vmem_limit_bytes=32 * 1024 * 1024
        ),
        name="powers_and_sums",
    )(start, links, link_weight, pool_slot.reshape(1, nodes))


def reduce_basis(gram_sum, mixed_sum, block_size):
    highest = lax.Precision.HIGHEST
    basis_size = gram_sum.shape[0]
    lower_fac = jnp.linalg.cholesky(gram_sum)
    symmetric = 0.5 * (mixed_sum + mixed_sum.T)
    halfway = lax.linalg.triangular_solve(lower_fac, symmetric, left_side=True, lower=True)
    reduced = lax.linalg.triangular_solve(lower_fac, halfway.T, left_side=True, lower=True)
    shifted = 0.5 * (reduced + jnp.eye(basis_size, dtype=jnp.float32))
    filtered = jnp.dot(shifted, shifted, precision=highest)
    filtered = jnp.dot(filtered, filtered, precision=highest)
    start_coords = lower_fac.T[:, :block_size]
    tilted = jnp.dot(filtered, start_coords, precision=highest)
    factor = jnp.linalg.cholesky(jnp.dot(tilted.T, tilted, precision=highest))
    orthonormal = lax.linalg.triangular_solve(factor, tilted.T, left_side=True, lower=True).T
    coeffs = lax.linalg.triangular_solve(
        lower_fac, orthonormal, left_side=True, lower=True, transpose_a=True
    )
    ritz_part = jnp.dot(
        orthonormal.T, jnp.dot(reduced, orthonormal, precision=highest), precision=highest
    )
    return (coeffs, ritz_part)


def per_device(start, links, link_weight, pool_slot):
    highest = lax.Precision.HIGHEST
    block, nodes = start.shape
    node_count = nodes * lax.axis_size("dom") * lax.axis_size("sub")
    one, two, sums = powers_and_sums(start, links, link_weight, pool_slot)
    sums = sums / node_count
    moments = [
        sums[r * block : (r + 1) * block, c * block : (c + 1) * block]
        for r in range(3)
        for c in range(2)
    ]
    moments = [0.5 * (m + m.T) for m in moments]

    def hankel(first, size):
        return jnp.concatenate(
            [
                jnp.concatenate([moments[first + i + j] for j in range(size)], axis=1)
                for i in range(size)
            ],
            axis=0,
        )

    coeffs_one, theta_one = reduce_basis(hankel(0, 2), hankel(1, 2), block)
    head, tail = coeffs_one[:block], coeffs_one[block:]
    nothing = jnp.zeros_like(head)
    residual = jnp.concatenate([nothing, head, tail], axis=0) - jnp.dot(
        jnp.concatenate([head, tail, nothing], axis=0), theta_one, precision=highest
    )
    basis_two = jnp.concatenate(
        [
            jnp.concatenate([head, tail, nothing], axis=0),
            residual,
            jnp.concatenate([nothing, tail, nothing], axis=0),
        ],
        axis=1,
    )

    def project(moment_matrix):
        right = jnp.dot(moment_matrix, basis_two, precision=highest)
        return jnp.dot(basis_two.T, right, precision=highest)

    coeffs_two, ritz_block = reduce_basis(project(hankel(0, 3)), project(hankel(1, 3)), block)
    weights = jnp.dot(basis_two, coeffs_two, precision=highest)
    eigen_block = jnp.dot(
        weights.T, jnp.concatenate([start, one, two], axis=0), precision=highest
    )
    return (eigen_block, ritz_block)


def solution(mesh):
    placed = (
        P(None, ("dom", "sub")),
        P(None, ("dom", "sub")),
        P(None, ("dom", "sub")),
        P(("dom", "sub")),
    )
    return jax.shard_map(
        per_device,
        mesh=mesh,
        in_specs=placed,
        out_specs=(P(None, ("dom", "sub")), P()),
        check_vma=False,
    )
```

time: 1410 us -> 197 us (0.14)
  waiting for transfers between devices: 1180 us -> 0 us
  Pallas kernels: 0 us -> 81.3 us
  local copies, waits for them, and re-layouts: 52.5 us -> 4.07 us
  other arithmetic: 122 us -> 96.2 us
  starting transfers between devices: 16.2 us -> 0 us
    psum x5 -> x0, waiting for transfers between devices: 1170 us -> none  [the longest x2 940 us: ritz_sums(): lax.psum((products(basis, basis), products(basis, jnp.concatenate(stacked...]
    pallas_call x0 -> x1, Pallas kernels: none -> 81.3 us  [powers_and_sums(): pl.pallas_call(functools.partial(sums_kernel, n_dom, n_sub), out_shape=(v...]
    gather x3 -> x0, local copies, waits for them, and re-layouts: 47.8 us -> none  [affinity(): jnp.take(lookup, flat_links, axis=1)]
    ppermute x6 -> x0, starting transfers between devices: 15.8 us -> none  [the longest x3 12 us: padded(): lax.ppermute(tail, axis, [(i, (i + 1) % count) for i in range(ends)])]
  transfers between devices with their start and end apart: 11 -> 0, of which waited for: 11 -> 0; matrix products, arithmetic and copies ran while one was open for 0% -> 0% of each run, Pallas kernels for 0% -> 0%
where the time goes in v1:
time: 197 us; the launch traced here: 196 us
  other arithmetic  96.2 us (49%)
  Pallas kernels  81.3 us (41%)
  matrix products  12.2 us (6%)
  local copies, waits for them, and re-layouts  4.07 us (2%)
  between operations  2.49 us (1%)
    pallas_call x1, Pallas kernels, powers_and_sums(): pl.pallas_call(functools.partial(sums_kernel, n_dom, n_sub), out_shape=(v...  81.3 us
    another operation x10, other arithmetic, reduce_basis(): lower_fac = jnp.linalg.cholesky(gram_sum)  41.1 us
    another operation x6, other arithmetic, reduce_basis(): lax.linalg.triangular_solve(lower_fac, orthonormal, left_side=True, lower...  29.9 us
    another operation x6, other arithmetic, reduce_basis(): factor = jnp.linalg.cholesky(jnp.dot(tilted.T, tilted, precision=highest))  13 us
    another operation x4, other arithmetic, reduce_basis(): lax.linalg.triangular_solve(factor, tilted.T, left_side=True, lower=True)  11.1 us

profile of v1, /device:TPU:1, one launch (start us, length us, event | category | flops | bytes accessed | tf_op | source)
XLA Modules:
  0.0 196.2 jit_solution(8041948896625334867)
XLA Ops:
  0.7 0.8 copy-done
  1.5 0.7 copy-done.1
  2.2 0.7 copy-done.2
  2.9 81.3 %powers_and_sums.1 = (f32[64,256]{1,0:T(8,128)S(1)}, f32[64,256]{1,0:T(8,128)S(1)}, f32[192,128]{1,0:T(8,128)S(1)}) custom-call(f32[64,256]{1,0:T(8,128)S(1)} %copy-done, s32[20,256]{1,0:T(8,128)S(1)} %copy-done.1, f32[20,256]{1,0:T(8,128)S(1)} %copy-done.2, s32[1,256]{1,0:T(1,128)S(1)} %bitcast.136), custom_call_target="tpu_custom_call" | custom-call | tf_op jit(solution)/shard_map/powers_and_sums/pallas_call | solution.py:267
  85.8 11.7 %cholesky.80 = f32[128,128]{1,0:T(8,128)S(1)} custom-call(f32[128,128]{1,0:T(8,128)S(1)} %copy.14), custom_call_target="Cholesky" | custom-call | tf_op jit(solution)/shard_map/jit(cholesky)/cholesky | solution.py:307
  97.5 0.6 compare_reduce_fusion.4
  98.2 0.7 fusion.78
  98.8 9.8 %custom-call.34 = f32[1,128,128]{1,2,0:T(8,128)S(1)} custom-call(f32[1,128,128]{2,1,0:T(8,128)S(1)} %get-tuple-element.73), custom_call_target="InvertDiagBlocksLowerTriangular" | custom-call | tf_op jit(solution)/shard_map/triangular_solve | solution.py:318
  110.3 5.8 %cholesky.177 = f32[64,64]{1,0:T(8,128)S(1)} custom-call(f32[64,64]{1,0:T(8,128)S(1)} %fusion.93), custom_call_target="Cholesky" | custom-call | tf_op jit(solution)/shard_map/jit(cholesky)/cholesky | solution.py:316
  116.2 0.6 compare_reduce_fusion.1
  116.8 0.7 fusion.79
  117.5 4.9 %custom-call.35 = f32[1,64,64]{1,2,0:T(8,128)S(1)} custom-call(f32[1,64,64]{2,1,0:T(8,128)S(1)} %fusion.79), custom_call_target="InvertDiagBlocksLowerTriangular" | custom-call | tf_op jit(solution)/shard_map/triangular_solve | solution.py:317
  123.5 0.7 fusion.18
  124.2 0.6 fusion.114
  124.8 0.7 fusion
  125.5 0.8 fusion.115
  126.5 11.7 %cholesky.92 = f32[128,128]{1,0:T(8,128)S(1)} custom-call(f32[128,128]{1,0:T(8,128)S(1)} %cholesky.197), custom_call_target="Cholesky" | custom-call | tf_op jit(solution)/shard_map/jit(cholesky)/cholesky | solution.py:307
  138.3 0.6 compare_reduce_fusion.3
  138.9 9.8 %custom-call.36 = f32[1,128,128]{1,2,0:T(8,128)S(1)} custom-call(f32[1,128,128]{2,1,0:T(8,128)S(1)} %get-tuple-element.71), custom_call_target="InvertDiagBlocksLowerTriangular" | custom-call | tf_op jit(solution)/shard_map/jit(cholesky)/cholesky | solution.py:307
  149.1 5.8 %cholesky.147 = f32[64,64]{1,0:T(8,128)S(1)} custom-call(f32[64,64]{1,0:T(8,128)S(1)} %convolution_subtract_fusion.4), custom_call_target="Cholesky" | custom-call | tf_op jit(solution)/shard_map/jit(cholesky)/cholesky | solution.py:307
  155.0 0.6 compare_reduce_fusion.2
  157.1 19.9 %custom-call.37 = f32[2,128,128]{1,2,0:T(8,128)S(1)} custom-call(f32[2,128,128]{2,1,0:T(8,128)S(1)} %pad_maximum_fusion.3), custom_call_target="InvertDiagBlocksLowerTriangular" | custom-call | tf_op jit(solution)/shard_map/triangular_solve | solution.py:318
  177.2 0.4 fusion.53
  177.9 0.3 fusion.99
  178.3 0.4 fusion.51
  180.7 5.8 %cholesky.188 = f32[64,64]{1,0:T(8,128)S(1)} custom-call(f32[64,64]{1,0:T(8,128)S(1)} %fusion.88), custom_call_target="Cholesky" | custom-call | tf_op jit(solution)/shard_map/jit(cholesky)/cholesky | solution.py:316
  186.6 0.6 compare_reduce_fusion
  187.2 0.7 fusion.80
  187.9 4.9 %custom-call.38 = f32[1,64,64]{1,2,0:T(8,128)S(1)} custom-call(f32[1,64,64]{2,1,0:T(8,128)S(1)} %fusion.80), custom_call_target="InvertDiagBlocksLowerTriangular" | custom-call | tf_op jit(solution)/shard_map/triangular_solve | solution.py:317
  193.4 0.8 fusion.123
  194.9 0.4 fusion.55
  195.2 1.0 fusion.36
  (80 shorter events, 8.6 us)
Async XLA Ops:
  0.6 0.8 copy-start
  0.7 0.8 copy-start.3
  1.5 0.7 copy-start.1
  2.2 0.7 copy-start.2

commit v2 on v1

--- a/solution.py
+++ b/solution.py
@@ -14,6 +14,7 @@
 ROUNDS = 3
 BUILD_ROWS = 64
 N_Z = 12
+SUBLANES = 8
 
 
 def split(values):
@@ -301,76 +302,170 @@
     )(start, links, link_weight, pool_slot.reshape(1, nodes))
 
 
-def reduce_basis(gram_sum, mixed_sum, block_size):
-    highest = lax.Precision.HIGHEST
-    basis_size = gram_sum.shape[0]
-    lower_fac = jnp.linalg.cholesky(gram_sum)
-    symmetric = 0.5 * (mixed_sum + mixed_sum.T)
-    halfway = lax.linalg.triangular_solve(lower_fac, symmetric, left_side=True, lower=True)
-    reduced = lax.linalg.triangular_solve(lower_fac, halfway.T, left_side=True, lower=True)
-    shifted = 0.5 * (reduced + jnp.eye(basis_size, dtype=jnp.float32))
-    filtered = jnp.dot(shifted, shifted, precision=highest)
-    filtered = jnp.dot(filtered, filtered, precision=highest)
-    start_coords = lower_fac.T[:, :block_size]
-    tilted = jnp.dot(filtered, start_coords, precision=highest)
-    factor = jnp.linalg.cholesky(jnp.dot(tilted.T, tilted, precision=highest))
-    orthonormal = lax.linalg.triangular_solve(factor, tilted.T, left_side=True, lower=True).T
-    coeffs = lax.linalg.triangular_solve(
-        lower_fac, orthonormal, left_side=True, lower=True, transpose_a=True
-    )
-    ritz_part = jnp.dot(
-        orthonormal.T, jnp.dot(reduced, orthonormal, precision=highest), precision=highest
-    )
-    return (coeffs, ritz_part)
+def product(left, right, dims):
+    return lax.dot_general(
+        left, right, (dims, ((), ())),
+        precision=lax.Precision.HIGHEST, preferred_element_type=jnp.float32,
+    )
+
+
+def nn(left, right):
+    return product(left, right, ((1,), (0,)))
+
+
+def nt(left, right):
+    return product(left, right, ((1,), (1,)))
+
+
+def tn(left, right):
+    return product(left, right, ((0,), (0,)))
+
+
+def eye(size):
+    rows = lax.broadcasted_iota(jnp.int32, (size, size), 0)
+    cols = lax.broadcasted_iota(jnp.int32, (size, size), 1)
+    return jnp.where(rows == cols, 1.0, 0.0)
+
+
+def mean_with_transpose(matrix):
+    return 0.5 * (matrix + matrix.T)
+
+
+def cholesky_and_inverse(matrix):
+    size = matrix.shape[0]
+    tiles = size // SUBLANES
+    wide = jnp.concatenate([matrix, eye(size)], axis=1)
+    shape = (SUBLANES, 2 * size)
+    rows = [wide[SUBLANES * i : SUBLANES * (i + 1), :] for i in range(tiles)]
+    ids = lax.broadcasted_iota(jnp.int32, shape, 0)
+    pivots = []
+    for t in range(tiles):
+        first = SUBLANES * t
+        spread = {
+            (i, k): jnp.broadcast_to(rows[i][:, first + k : first + k + 1], shape)
+            for i in range(t, tiles)
+            for k in range(SUBLANES)
+        }
+        for k in range(SUBLANES):
+            inverse = 1.0 / jnp.broadcast_to(spread[t, k][k : k + 1, :], shape)
+            row = jnp.broadcast_to(rows[t][k : k + 1, :], shape) * inverse
+            ahead = {
+                c: jnp.broadcast_to(spread[t, c][k : k + 1, :], shape) * inverse
+                for c in range(k + 1, SUBLANES)
+            }
+            for i in range(t, tiles):
+                factor = spread[i, k]
+                if i == t:
+                    factor = jnp.where(ids > k, factor, 0.0)
+                rows[i] = rows[i] - factor * row
+                for c in range(k + 1, SUBLANES):
+                    spread[i, c] = spread[i, c] - factor * ahead[c]
+        pivot = spread[t, 0]
+        for k in range(1, SUBLANES):
+            pivot = jnp.where(ids == k, spread[t, k], pivot)
+        rows[t] = rows[t] * lax.rsqrt(pivot)
+    result = jnp.concatenate(rows, axis=0)
+    upper = result[:, :size]
+    row_ids = lax.broadcasted_iota(jnp.int32, (size, size), 0)
+    col_ids = lax.broadcasted_iota(jnp.int32, (size, size), 1)
+    return jnp.where(col_ids >= row_ids, upper, 0.0), result[:, size:]
+
+
+def filtered(reduced, first):
+    half = 0.5 * (reduced + eye(reduced.shape[0]))
+    square = nn(half, half)
+    return nn(square, first(square))
+
+
+def ritz_step_one(m0, m1, m2, m3):
+    block = m0.shape[0]
+    zero = jnp.zeros_like(m0)
+    upper, inv_first = cholesky_and_inverse(m0)
+    below = nt(m1, inv_first)
+    _, inv_second = cholesky_and_inverse(m2 - nt(below, below))
+    inv_below = -nn(inv_second, nn(below, inv_first))
+    inverse = jnp.concatenate(
+        [
+            jnp.concatenate([inv_first, zero], axis=1),
+            jnp.concatenate([inv_below, inv_second], axis=1),
+        ],
+        axis=0,
+    )
+    mixed = jnp.concatenate(
+        [jnp.concatenate([m1, m2], axis=1), jnp.concatenate([m2, m3], axis=1)], axis=0
+    )
+    reduced = nt(nn(inverse, mixed), inverse)
+    tilted = filtered(reduced, lambda square: nn(square[:, :block], upper))
+    _, normal = cholesky_and_inverse(tn(tilted, tilted))
+    orthonormal = nt(tilted, normal)
+    coeffs = tn(inverse, orthonormal)
+    theta = tn(orthonormal, nn(reduced, orthonormal))
+    return coeffs[:block], coeffs[block:], theta
+
+
+def ritz_step_two(moments, head, tail, theta):
+    block = head.shape[0]
+    zero = jnp.zeros_like(head)
+
+    def hankel(first):
+        return jnp.concatenate(
+            [
+                jnp.concatenate([moments[first + i + j] for j in range(3)], axis=1)
+                for i in range(3)
+            ],
+            axis=0,
+        )
+
+    gram, mixed = hankel(0), hankel(1)
+    current = jnp.concatenate([head, tail, zero], axis=0)
+    search = jnp.concatenate([zero, tail, zero], axis=0)
+    residual = jnp.concatenate([zero, head, tail], axis=0) - nn(current, theta)
+    search = search - nn(current, tn(current, nn(gram, search)))
+    _, normal = cholesky_and_inverse(tn(search, nn(gram, search)))
+    search = nt(search, normal)
+    residual = residual - nn(search, tn(search, nn(gram, residual)))
+    _, normal = cholesky_and_inverse(tn(residual, nn(gram, residual)))
+    residual = nt(residual, normal)
+    basis = jnp.concatenate([current, search, residual], axis=1)
+    reduced = tn(basis, nn(mixed, basis))
+    tilted = filtered(reduced, lambda square: square[:, :block])
+    _, normal = cholesky_and_inverse(tn(tilted, tilted))
+    orthonormal = nt(tilted, normal)
+    ritz = tn(orthonormal, nn(reduced, orthonormal))
+    return nn(basis, orthonormal), ritz
+
+
+def ritz_kernel(scale, sums_ref, start_ref, one_ref, two_ref, eigen_ref, ritz_ref):
+    block = start_ref.shape[0]
+    moments = [
+        mean_with_transpose(
+            sums_ref[r * block : (r + 1) * block, c * block : (c + 1) * block] * scale
+        )
+        for r in range(3)
+        for c in range(2)
+    ]
+    head, tail, theta = ritz_step_one(*moments[:4])
+    weights, ritz = ritz_step_two(moments, head, tail, theta)
+    ritz_ref[...] = ritz
+    powers = jnp.concatenate([start_ref[...], one_ref[...], two_ref[...]], axis=0)
+    eigen_ref[...] = tn(weights, powers)
 
 
 def per_device(start, links, link_weight, pool_slot):
-    highest = lax.Precision.HIGHEST
     block, nodes = start.shape
     node_count = nodes * lax.axis_size("dom") * lax.axis_size("sub")
     one, two, sums = powers_and_sums(start, links, link_weight, pool_slot)
-    sums = sums / node_count
-    moments = [
-        sums[r * block : (r + 1) * block, c * block : (c + 1) * block]
-        for r in range(3)
-        for c in range(2)
-    ]
-    moments = [0.5 * (m + m.T) for m in moments]
-
-    def hankel(first, size):
-        return jnp.concatenate(
-            [
-                jnp.concatenate([moments[first + i + j] for j in range(size)], axis=1)
-                for i in range(size)
-            ],
-            axis=0,
-        )
-
-    coeffs_one, theta_one = reduce_basis(hankel(0, 2), hankel(1, 2), block)
-    head, tail = coeffs_one[:block], coeffs_one[block:]
-    nothing = jnp.zeros_like(head)
-    residual = jnp.concatenate([nothing, head, tail], axis=0) - jnp.dot(
-        jnp.concatenate([head, tail, nothing], axis=0), theta_one, precision=highest
-    )
-    basis_two = jnp.concatenate(
-        [
-            jnp.concatenate([head, tail, nothing], axis=0),
-            residual,
-            jnp.concatenate([nothing, tail, nothing], axis=0),
-        ],
-        axis=1,
-    )
-
-    def project(moment_matrix):
-        right = jnp.dot(moment_matrix, basis_two, precision=highest)
-        return jnp.dot(basis_two.T, right, precision=highest)
-
-    coeffs_two, ritz_block = reduce_basis(project(hankel(0, 3)), project(hankel(1, 3)), block)
-    weights = jnp.dot(basis_two, coeffs_two, precision=highest)
-    eigen_block = jnp.dot(
-        weights.T, jnp.concatenate([start, one, two], axis=0), precision=highest
-    )
-    return (eigen_block, ritz_block)
+    return pl.pallas_call(
+        functools.partial(ritz_kernel, 1.0 / node_count),
+        out_shape=(
+            jax.ShapeDtypeStruct((block, nodes), jnp.float32),
+            jax.ShapeDtypeStruct((block, block), jnp.float32),
+        ),
+        in_specs=[pl.BlockSpec(memory_space=VMEM)] * 4,
+        out_specs=(pl.BlockSpec(memory_space=VMEM),) * 2,
+        compiler_params=pltpu.CompilerParams(vmem_limit_bytes=32 * 1024 * 1024),
+        name="ritz_steps",
+    )(sums, start, one, two)
 
 
 def solution(mesh):

time: 197 us -> 107 us (0.54)
  other arithmetic: 96.2 us -> 0 us
  Pallas kernels: 81.3 us -> 103 us
  matrix products: 12.2 us -> 0 us
    another operation x26 -> x0, other arithmetic: 95.1 us -> none  [the longest x10 41.1 us: reduce_basis(): lower_fac = jnp.linalg.cholesky(gram_sum)]
    pallas_call x0 -> x1, Pallas kernels: none -> 21.5 us  [per_device(): pl.pallas_call(functools.partial(ritz_kernel, 1.0 / node_count), out_shap...]
    dot_general x19 -> x0, matrix products: 7.96 us -> none  [the longest x2 1.46 us: project(): return jnp.dot(basis_two.T, right, precision=highest)]
    another operation x16 -> x0, matrix products: 4.2 us -> none  [the longest x4 1.32 us: reduce_basis(): lax.linalg.triangular_solve(lower_fac, symmetric, left_side=True, lower=T...]
where the time goes in v2:
time: 107 us
  Pallas kernels  103 us (96%)
  local copies, waits for them, and re-layouts  2.98 us (3%)
    pallas_call x1, Pallas kernels, powers_and_sums(): pl.pallas_call(functools.partial(sums_kernel, n_dom, n_sub), out_shape=(v...  81.4 us
    pallas_call x1, Pallas kernels, per_device(): pl.pallas_call(functools.partial(ritz_kernel, 1.0 / node_count), out_shap...  21.5 us
    unnamed x8, local copies, waits for them, and re-layouts  2.98 us

profile of v2, /device:TPU:1, one launch (start us, length us, event | category | flops | bytes accessed | tf_op | source)
XLA Modules:
  0.0 106.6 jit_solution(3743739567830458236)
XLA Ops:
  0.6 0.0 copy-start.3
  0.6 0.7 copy-done.3
  1.3 0.0 copy-start
  1.3 0.8 copy-done
  2.2 0.0 copy-start.1
  2.2 0.7 copy-done.1
  2.9 0.0 copy-start.2
  2.9 0.7 copy-done.2
  3.6 81.4 %powers_and_sums.1 = (f32[64,256]{1,0:T(8,128)S(1)}, f32[64,256]{1,0:T(8,128)S(1)}, f32[192,128]{1,0:T(8,128)S(1)}) custom-call(f32[64,256]{1,0:T(8,128)S(1)} %copy-done, s32[20,256]{1,0:T(8,128)S(1)} %copy-done.1, f32[20,256]{1,0:T(8,128)S(1)} %copy-done.2, s32[1,256]{1,0:T(1,128)S(1)} %bitcast.1), custom_call_target="tpu_custom_call" | custom-call | tf_op jit(solution)/shard_map/powers_and_sums/pallas_call | solution.py:268
  85.0 21.5 %ritz_steps.1 = (f32[64,256]{1,0:T(8,128)}, f32[64,64]{1,0:T(8,128)}) custom-call(f32[192,128]{1,0:T(8,128)S(1)} %get-tuple-element.5.sums_ref, f32[64,256]{1,0:T(8,128)S(1)} %copy-done, f32[64,256]{1,0:T(8,128)S(1)} %get-tuple-element.6.one_ref, f32[64,256]{1,0:T(8,128)S(1)} %get-tuple-element.7.two_ref), custom_call_target="tpu_custom_call" | custom-call | tf_op jit(solution)/shard_map/ritz_steps/pallas_call | solution.py:458
Async XLA Ops:
  0.6 0.7 copy-start.3
  1.3 0.8 copy-start
  2.2 0.7 copy-start.1
  2.9 0.7 copy-start.2

commit v3 on v1

v3 whole, which is shorter than its diff:
```python
import functools

import jax
import jax.numpy as jnp
from jax import lax
from jax.experimental import pallas as pl
from jax.experimental.pallas import tpu as pltpu
from jax.sharding import PartitionSpec as P

MESH = pl.DeviceIdType.MESH
VMEM = pltpu.VMEM
DMA = pltpu.SemaphoreType.DMA
SLOT_DEV = 64
ROUNDS = 3
BUILD_ROWS = 64
N_Z = 12
SUBLANES = 8
LANES = 128
WIDTHS = (2 * LANES, LANES, LANES)


def split(values):
    high = values.astype(jnp.bfloat16)
    low = (values - high.astype(jnp.float32)).astype(jnp.bfloat16)
    return high, low


def product(left, right, dims):
    return lax.dot_general(
        left, right, (dims, ((), ())),
        precision=lax.Precision.HIGHEST, preferred_element_type=jnp.float32,
    )


def nn(left, right):
    return product(left, right, ((1,), (0,)))


def nt(left, right):
    return product(left, right, ((1,), (1,)))


def tn(left, right):
    return product(left, right, ((0,), (0,)))


def eye(size):
    rows = lax.broadcasted_iota(jnp.int32, (size, size), 0)
    cols = lax.broadcasted_iota(jnp.int32, (size, size), 1)
    return jnp.where(rows == cols, 1.0, 0.0)


def mean_with_transpose(matrix):
    return 0.5 * (matrix + matrix.T)


def cholesky_and_inverse(matrix):
    size = matrix.shape[0]
    width = 2 * size
    rows = jnp.concatenate([matrix, eye(size)], axis=1)
    ids = lax.broadcasted_iota(jnp.int32, (size, width), 0)
    done = []
    for first in range(0, size, SUBLANES):
        left = size - first
        tile = (SUBLANES, width)
        spread = [
            jnp.broadcast_to(rows[:, first + k : first + k + 1], (left, width))
            for k in range(SUBLANES)
        ]
        for k in range(SUBLANES):
            inverse = 1.0 / jnp.broadcast_to(spread[k][k : k + 1, :], tile)
            factor = jnp.where(ids[:left] > k, spread[k], 0.0)

            def eliminate(values):
                pivot_row = jnp.broadcast_to(values[k : k + 1, :], tile) * inverse
                return values - factor * jnp.concatenate([pivot_row] * (left // SUBLANES), axis=0)

            rows = eliminate(rows)
            for c in range(k + 1, SUBLANES):
                spread[c] = eliminate(spread[c])
        pivot = spread[0][:SUBLANES]
        for k in range(1, SUBLANES):
            pivot = jnp.where(ids[:SUBLANES] == k, spread[k][:SUBLANES], pivot)
        done.append(rows[:SUBLANES] * lax.rsqrt(pivot))
        rows = rows[SUBLANES:]
    result = jnp.concatenate(done, axis=0)
    upper = result[:, :size]
    row_ids = lax.broadcasted_iota(jnp.int32, (size, size), 0)
    col_ids = lax.broadcasted_iota(jnp.int32, (size, size), 1)
    return jnp.where(col_ids >= row_ids, upper, 0.0), result[:, size:]


def blocks(rows):
    return jnp.concatenate([jnp.concatenate(row, axis=1) for row in rows], axis=0)


def filtered(reduced, first):
    half = 0.5 * (reduced + eye(reduced.shape[0]))
    square = nn(half, half)
    return nn(square, first(square))


def factor_one(m0, m1, m2):
    upper, first = cholesky_and_inverse(m0)
    below = nt(m1, first)
    return upper, first, below, m2 - nt(below, below)


def inverse_one(first, below, rest):
    _, second = cholesky_and_inverse(rest)
    corner = -nn(second, nn(below, first))
    return blocks([[first, jnp.zeros_like(first)], [corner, second]])


def filter_one(inverse, upper, m1, m2, m3):
    block = upper.shape[0]
    reduced = nt(nn(inverse, blocks([[m1, m2], [m2, m3]])), inverse)
    tilted = filtered(reduced, lambda square: nn(square[:, :block], upper))
    return reduced, tilted, tn(tilted, tilted)


def ritz_one(inverse, reduced, tilted, gram):
    _, normal = cholesky_and_inverse(gram)
    orthonormal = nt(tilted, normal)
    coeffs = tn(inverse, orthonormal)
    return coeffs, tn(orthonormal, nn(reduced, orthonormal))


def basis_two(coeffs, theta, moments):
    m0, m1, m2, m3, m4 = moments
    block = theta.shape[0]
    head, tail = coeffs[:block], coeffs[block:]
    zero = jnp.zeros_like(head)
    gram = blocks([[m0, m1, m2], [m1, m2, m3], [m2, m3, m4]])
    current = jnp.concatenate([head, tail, zero], axis=0)
    search = jnp.concatenate([zero, tail, zero], axis=0)
    residual = jnp.concatenate([zero, head, tail], axis=0) - nn(current, theta)
    gram_current = nn(gram, current)
    search = search - nn(current, tn(gram_current, search))
    gram_search = nn(gram, search)
    _, normal = cholesky_and_inverse(tn(search, gram_search))
    search = nt(search, normal)
    gram_search = nt(gram_search, normal)
    residual = residual - nn(search, tn(gram_search, residual))
    _, normal = cholesky_and_inverse(tn(residual, nn(gram, residual)))
    residual = nt(residual, normal)
    basis = jnp.concatenate([current, search, residual], axis=1)
    mixed = blocks([[m1, m2, m3], [m2, m3, m4], [m3, m4, zero]])
    return basis, tn(basis, nn(mixed, basis))


def ritz_kernel(scale, sums_ref, basis_ref, partial_ref, rotated_ref, eigen_ref, ritz_ref):
    block = ritz_ref.shape[0]
    last = mean_with_transpose(sums_ref[:, :block] * scale)
    tail = basis_ref[2 * block :, 2 * block :]
    zero = jnp.zeros((block, block), jnp.float32)
    corner = tn(tail, nn(last, tail))
    reduced = partial_ref[...] + blocks(
        [[zero, zero, zero], [zero, zero, zero], [zero, zero, corner]]
    )
    tilted = filtered(reduced, lambda square: square[:, :block])
    _, normal = cholesky_and_inverse(tn(tilted, tilted))
    turned = tn(tilted, rotated_ref[...])
    projected = tn(tilted, nn(reduced, tilted))
    eigen_ref[...] = nn(normal, turned)
    ritz_ref[...] = nt(nn(normal, projected), normal)


def each(low, high, body):
    lax.fori_loop(low, high, lambda k, c: (body(k), c)[1], 0)


def far_first(count):
    return sorted(range(1, count), key=lambda k: -min(k, count - k))


def sums_kernel(
    n_dom,
    n_sub,
    start_ref,
    links_ref,
    weight_ref,
    slot_ref,
    basis_ref,
    partial_ref,
    rotated_ref,
    last_ref,
    one_ref,
    two_ref,
    root_ref,
    place_ref,
    table_hi,
    table_lo,
    contrib,
    gathered,
    pools,
    own_a,
    own_b,
    own_c,
    part_a,
    part_b,
    part_c,
    z_a,
    z_b,
    z_c,
    y_a,
    y_b,
    y_c,
    sums_a,
    sums_b,
    rs_send,
    rs_recv,
    ag_send,
    ag_recv,
    part_send,
    part_recv,
    z_send,
    z_recv,
    y_send,
    y_recv,
    out_send,
    out_recv,
):
    dom = lax.axis_index("dom")
    sub = lax.axis_index("sub")
    n_y = n_dom // N_Z
    row = lax.div(dom, N_Z)
    col = lax.rem(dom, N_Z)
    block = start_ref.shape[0]
    nodes = start_ref.shape[1]
    slots = place_ref.shape[0]
    share = block // n_sub
    scale = 1.0 / (nodes * n_dom * n_sub)
    own = (own_a, own_b, own_c)
    part_in = (part_a, part_b, part_c)
    z_in = (z_a, z_b, z_c)
    y_in = (y_a, y_b, y_c)
    sums = (sums_a, sums_b, last_ref)

    def sub_peer(k):
        return lax.rem(sub + k, n_sub)

    def dom_peer(area):
        return lax.rem(dom + (area + n_dom - 1), n_dom)

    def z_peer(k):
        return lax.rem(col + k, N_Z)

    def y_peer(k):
        return lax.rem(row + k, n_y)

    def remote(src, dst, send, recv, d, s):
        return pltpu.make_async_remote_copy(
            src_ref=src, dst_ref=dst, send_sem=send, recv_sem=recv,
            device_id=(d, s), device_id_type=MESH,
        )

    barrier = pltpu.get_barrier_semaphore()

    def greet(d, s):
        pl.semaphore_signal(barrier, inc=1, device_id=(d, s), device_id_type=MESH)

    for k in far_first(n_sub):
        greet(dom, sub_peer(k))
    for k in range(n_sub):
        greet(dom_peer(0), k)
        greet(dom_peer(2), k)
    for k in far_first(N_Z):
        greet(row * N_Z + z_peer(k), sub)
    for k in far_first(n_y):
        greet(y_peer(k) * N_Z + col, sub)

    def rs_copy(j, peer, at):
        return remote(contrib.at[j, peer], gathered.at[j, at],
                      rs_send.at[j, peer], rs_recv.at[j, at], dom, peer)

    def ag_copy(j, to, peer, area, at):
        return remote(pools.at[j, 1, sub], pools.at[j, area, at],
                      ag_send.at[j, to, peer], ag_recv.at[j, area, at], dom_peer(to), peer)

    def rows_of(p):
        return pl.ds(pl.multiple_of(p * share, share), share)

    def part_copy(b, peer, at):
        return remote(own[b].at[rows_of(peer)], part_in[b].at[at],
                      part_send.at[b, peer], part_recv.at[b, at], dom, peer)

    def z_copy(b, peer, at):
        return remote(z_in[b].at[col], z_in[b].at[at],
                      z_send.at[b, peer], z_recv.at[b, at], row * N_Z + peer, sub)

    def y_copy(b, peer, at):
        return remote(y_in[b].at[row], y_in[b].at[at],
                      y_send.at[b, peer], y_recv.at[b, at], peer * N_Z + col, sub)

    def out_copy(b, peer, at):
        return remote(sums[b].at[rows_of(sub)], sums[b].at[rows_of(at)],
                      out_send.at[b, peer], out_recv.at[b, at], dom, peer)

    def total(ref, count):
        result = ref[0]
        for k in range(1, count):
            result = result + ref[k]
        return result

    def sum_begin(b):
        for k in far_first(n_sub):
            part_copy(b, sub_peer(k), sub).start()
        part_in[b][sub] = own[b][rows_of(sub), :]

    def sum_along_z(b):
        for k in far_first(n_sub)[::-1]:
            part_copy(b, sub_peer(k), sub_peer(k)).wait_recv()
        z_in[b][col] = total(part_in[b], n_sub)
        for k in far_first(N_Z):
            z_copy(b, z_peer(k), col).start()

    def sum_along_y(b):
        for k in far_first(N_Z)[::-1]:
            z_copy(b, z_peer(k), z_peer(k)).wait_recv()
        y_in[b][row] = total(z_in[b], N_Z)
        for k in far_first(n_y):
            y_copy(b, y_peer(k), row).start()

    def sum_back(b):
        for k in far_first(n_y)[::-1]:
            y_copy(b, y_peer(k), y_peer(k)).wait_recv()
        sums[b][rows_of(sub), :] = total(y_in[b], n_y)
        for k in far_first(n_sub):
            out_copy(b, sub_peer(k), sub).start()

    def sum_end(b):
        for k in far_first(n_sub)[::-1]:
            out_copy(b, sub_peer(k), sub_peer(k)).wait_recv()

    def sum_sent(b):
        each(1, n_sub, lambda k: part_copy(b, sub_peer(k), sub).wait_send())
        each(1, N_Z, lambda k: z_copy(b, z_peer(k), col).wait_send())
        each(1, n_y, lambda k: y_copy(b, y_peer(k), row).wait_send())
        each(1, n_sub, lambda k: out_copy(b, sub_peer(k), sub).wait_send())

    def rs_sent(j):
        each(1, n_sub, lambda k: rs_copy(j, sub_peer(k), sub).wait_send())

    def ag_sent(j):
        each(1, n_sub, lambda k: ag_copy(j, 1, sub_peer(k), 1, sub).wait_send())
        each(0, n_sub, lambda k: ag_copy(j, 0, k, 2, sub).wait_send())
        each(0, n_sub, lambda k: ag_copy(j, 2, k, 0, sub).wait_send())

    root_ref[...] = lax.rsqrt(jnp.sum(weight_ref[...], axis=0, keepdims=True))

    def place(i, carry):
        base = pl.multiple_of(i * BUILD_ROWS, BUILD_ROWS)
        ids = base + lax.broadcasted_iota(jnp.int32, (BUILD_ROWS, nodes), 0)
        place_ref[pl.ds(base, BUILD_ROWS), :] = jnp.where(
            ids == slot_ref[...], 1.0, 0.0
        ).astype(jnp.bfloat16)
        return carry

    lax.fori_loop(0, slots // BUILD_ROWS, place, 0)

    def build(i, carry):
        base = pl.multiple_of(i * BUILD_ROWS, BUILD_ROWS)
        ids = base + lax.broadcasted_iota(jnp.int32, (BUILD_ROWS, nodes), 0)
        summed = jnp.zeros((BUILD_ROWS, nodes), jnp.float32)
        for k in range(links_ref.shape[0]):
            summed = summed + jnp.where(
                ids == links_ref[k : k + 1, :], weight_ref[k : k + 1, :], 0.0
            )
        high, low = split(summed * root_ref[...])
        table_hi[pl.ds(base, BUILD_ROWS), :] = high
        table_lo[pl.ds(base, BUILD_ROWS), :] = low
        return carry

    def contribute(j, vectors):
        high, low = split(root_ref[...] * vectors)
        spread = lax.dot_general(
            jnp.concatenate([high, low], axis=0),
            place_ref[...],
            (((1,), (1,)), ((), ())),
            preferred_element_type=jnp.float32,
        )
        contrib[j] = (spread[:block] + spread[block:]).reshape(n_sub, share, slots)
        return high, low

    def apply(high, low, first, count):
        upper = jnp.dot(
            jnp.concatenate([high, low], axis=0),
            table_hi[first : first + count, :],
            preferred_element_type=jnp.float32,
        )
        lower = jnp.dot(
            high, table_lo[first : first + count, :], preferred_element_type=jnp.float32
        )
        return upper[:block] + upper[block:] + lower

    def affinity(j, vectors, while_reduced, while_gathered):
        high, low = contribute(j, vectors)
        if j == 0:
            pl.semaphore_wait(barrier, 3 * n_sub - 1 + N_Z - 1 + n_y - 1)
        for k in far_first(n_sub):
            rs_copy(j, sub_peer(k), sub).start()
        gathered[j, sub] = contrib[j, sub]
        while_reduced()
        summed = apply(high, low, 0, nodes)
        for k in far_first(n_sub)[::-1]:
            rs_copy(j, sub_peer(k), sub_peer(k)).wait_recv()
        pools[j, 1, sub] = total(gathered.at[j], n_sub)
        for k in far_first(n_sub) + [0]:
            ag_copy(j, 0, sub_peer(k), 2, sub).start()
            ag_copy(j, 2, sub_peer(k), 0, sub).start()
        for k in far_first(n_sub):
            ag_copy(j, 1, sub_peer(k), 1, sub).start()
        while_gathered()
        for k in range(1, n_sub):
            ag_copy(j, 1, sub_peer(k), 1, sub_peer(k)).wait_recv()
        for area in (1, 0, 2):
            if area != 1:
                for k in range(n_sub):
                    ag_copy(j, area, k, area, k).wait_recv()
            high, low = split(pools[j, area].reshape(block, slots))
            summed = summed + apply(high, low, nodes + area * slots, slots)
        return summed

    def build_table():
        lax.fori_loop(0, table_hi.shape[0] // BUILD_ROWS, build, 0)

    def moments_first():
        own_a[:, 0:block] = nt(start_ref[...], start_ref[...])
        own_a[:, 3 * block :] = jnp.zeros((block, block), jnp.float32)
        own_c[:, block:] = jnp.zeros((block, block), jnp.float32)
        rs_sent(0)

    def moments_second():
        own_a[:, block : 2 * block] = nt(start_ref[...], one_ref[...])
        own_a[:, 2 * block : 3 * block] = nt(one_ref[...], one_ref[...])
        sum_begin(0)
        ag_sent(0)

    def second_gathered():
        sum_along_z(0)
        rs_sent(1)

    def moments_third():
        own_b[:, 0:block] = nt(one_ref[...], two_ref[...])
        own_b[:, block:] = nt(two_ref[...], two_ref[...])
        sum_begin(1)
        sum_along_y(0)
        ag_sent(1)

    def third_gathered():
        sum_back(0)
        sum_along_z(1)
        rs_sent(2)

    one_ref[...] = affinity(0, start_ref[...], build_table, moments_first)
    two_ref[...] = affinity(1, one_ref[...], moments_second, second_gathered)
    three = affinity(2, two_ref[...], moments_third, third_gathered)
    own_c[:, 0:block] = nt(two_ref[...], three)

    def moment(b, c):
        return mean_with_transpose(sums[b][:, c * block : (c + 1) * block] * scale)

    sum_begin(2)
    sum_along_y(1)
    sum_end(0)
    m0, m1, m2 = moment(0, 0), moment(0, 1), moment(0, 2)
    upper, first, below, rest = factor_one(m0, m1, m2)
    sum_along_z(2)
    sum_back(1)
    inverse = inverse_one(first, below, rest)
    ag_sent(2)
    sum_sent(0)
    sum_end(1)
    m3, m4 = moment(1, 0), moment(1, 1)
    reduced, tilted, gram = filter_one(inverse, upper, m1, m2, m3)
    sum_along_y(2)
    coeffs, theta = ritz_one(inverse, reduced, tilted, gram)
    sum_back(2)
    basis, partial = basis_two(coeffs, theta, (m0, m1, m2, m3, m4))
    basis_ref[...] = basis
    partial_ref[...] = partial
    rotated_ref[...] = tn(
        basis, jnp.concatenate([start_ref[...], one_ref[...], two_ref[...]], axis=0)
    )
    sum_sent(1)
    sum_sent(2)
    sum_end(2)


def per_device(start, links, link_weight, pool_slot):
    n_dom = lax.axis_size("dom")
    n_sub = lax.axis_size("sub")
    n_y = n_dom // N_Z
    block, nodes = start.shape
    slots = SLOT_DEV * n_sub
    share = block // n_sub
    entries = nodes + 3 * slots
    f32 = jnp.float32
    vmem = pl.BlockSpec(memory_space=VMEM)
    limit = 32 * 1024 * 1024

    def array(*shape):
        return jax.ShapeDtypeStruct(shape, f32)

    def buffers(*shape):
        return [VMEM(shape + (width,), f32) for width in WIDTHS]

    basis, partial, rotated, last = pl.pallas_call(
        functools.partial(sums_kernel, n_dom, n_sub),
        out_shape=(
            array(3 * block, 3 * block),
            array(3 * block, 3 * block),
            array(3 * block, nodes),
            array(block, WIDTHS[2]),
        ),
        in_specs=[vmem] * 4,
        out_specs=(vmem,) * 4,
        scratch_shapes=[
            VMEM((block, nodes), f32),
            VMEM((block, nodes), f32),
            VMEM((1, nodes), f32),
            VMEM((slots, nodes), jnp.bfloat16),
            VMEM((entries, nodes), jnp.bfloat16),
            VMEM((entries, nodes), jnp.bfloat16),
            VMEM((ROUNDS, n_sub, share, slots), f32),
            VMEM((ROUNDS, n_sub, share, slots), f32),
            VMEM((ROUNDS, 3, n_sub, share, slots), f32),
            *buffers(block),
            *buffers(n_sub, share),
            *buffers(N_Z, share),
            *buffers(n_y, share),
            *buffers(block)[:2],
            DMA((ROUNDS, n_sub)),
            DMA((ROUNDS, n_sub)),
            DMA((ROUNDS, 3, n_sub)),
            DMA((ROUNDS, 3, n_sub)),
            *[DMA((len(WIDTHS), size)) for size in (n_sub, N_Z, n_y, n_sub) for _ in range(2)],
        ],
        compiler_params=pltpu.CompilerParams(
            collective_id=0, has_side_effects=True, vmem_limit_bytes=limit
        ),
        name="powers_and_sums",
    )(start, links, link_weight, pool_slot.reshape(1, nodes))
    return pl.pallas_call(
        functools.partial(ritz_kernel, 1.0 / (nodes * n_dom * n_sub)),
        out_shape=(array(block, nodes), array(block, block)),
        in_specs=[vmem] * 4,
        out_specs=(vmem,) * 2,
        compiler_params=pltpu.CompilerParams(vmem_limit_bytes=limit),
        name="ritz_steps",
    )(last, basis, partial, rotated)


def solution(mesh):
    placed = (
        P(None, ("dom", "sub")),
        P(None, ("dom", "sub")),
        P(None, ("dom", "sub")),
        P(("dom", "sub")),
    )
    return jax.shard_map(
        per_device,
        mesh=mesh,
        in_specs=placed,
        out_specs=(P(None, ("dom", "sub")), P()),
        check_vma=False,
    )
```

time: 197 us -> 96.3 us (0.49)
  other arithmetic: 96.2 us -> 0 us
  matrix products: 12.2 us -> 0 us
  Pallas kernels: 81.3 us -> 92.3 us
    another operation x26 -> x0, other arithmetic: 95.1 us -> none  [the longest x10 41.1 us: reduce_basis(): lower_fac = jnp.linalg.cholesky(gram_sum)]
    pallas_call x1 -> x2, Pallas kernels: 81.3 us -> 92.3 us  [the longest x1 87.7 us: per_device(): pl.pallas_call(functools.partial(sums_kernel, n_dom, n_sub), out_shape=(a...]
    dot_general x19 -> x0, matrix products: 7.96 us -> none  [the longest x2 1.46 us: project(): return jnp.dot(basis_two.T, right, precision=highest)]
    another operation x16 -> x0, matrix products: 4.2 us -> none  [the longest x4 1.32 us: reduce_basis(): lax.linalg.triangular_solve(lower_fac, symmetric, left_side=True, lower=T...]
where the time goes in v3:
time: 96.3 us; the launch traced here: 95.9 us
  Pallas kernels  92.3 us (96%)
  local copies, waits for them, and re-layouts  2.98 us (3%)
    pallas_call x1, Pallas kernels, per_device(): pl.pallas_call(functools.partial(sums_kernel, n_dom, n_sub), out_shape=(a...  87.7 us
    pallas_call x1, Pallas kernels, per_device(): pl.pallas_call(functools.partial(ritz_kernel, 1.0 / (nodes * n_dom * n_su...  4.63 us
    unnamed x8, local copies, waits for them, and re-layouts  2.98 us

profile of v3, /device:TPU:1, one launch (start us, length us, event | category | flops | bytes accessed | tf_op | source)
XLA Modules:
  0.0 95.9 jit_solution(7956924694798898910)
XLA Ops:
  0.6 0.0 copy-start.3
  0.6 0.7 copy-done.3
  1.3 0.0 copy-start
  1.3 0.8 copy-done
  2.2 0.0 copy-start.1
  2.2 0.7 copy-done.1
  2.9 0.0 copy-start.2
  2.9 0.7 copy-done.2
  3.6 87.7 %powers_and_sums.1 = (f32[192,192]{1,0:T(8,128)S(1)}, f32[192,192]{1,0:T(8,128)S(1)}, f32[192,256]{1,0:T(8,128)S(1)}, f32[64,128]{1,0:T(8,128)S(1)}) custom-call(f32[64,256]{1,0:T(8,128)S(1)} %copy-done, s32[20,256]{1,0:T(8,128)S(1)} %copy-done.1, f32[20,256]{1,0:T(8,128)S(1)} %copy-done.2, s32[1,256]{1,0:T(1,128)S(1)} %bitcast.1), custom_call_target="tpu_custom_call" | custom-call | tf_op jit(solution)/shard_map/powers_and_sums/pallas_call | solution.py:509
  91.3 4.6 %ritz_steps.1 = (f32[64,256]{1,0:T(8,128)}, f32[64,64]{1,0:T(8,128)}) custom-call(f32[64,128]{1,0:T(8,128)S(1)} %get-tuple-element.6.sums_ref, f32[192,192]{1,0:T(8,128)S(1)} %get-tuple-element.7.basis_ref, f32[192,192]{1,0:T(8,128)S(1)} %get-tuple-element.8.partial_ref, f32[192,256]{1,0:T(8,128)S(1)} %get-tuple-element.9.rotated_ref), custom_call_target="tpu_custom_call" | custom-call | tf_op jit(solution)/shard_map/ritz_steps/pallas_call | solution.py:545
Async XLA Ops:
  0.6 0.7 copy-start.3
  1.3 0.8 copy-start
  2.2 0.7 copy-start.1
  2.9 0.7 copy-start.2

commit v4 on v3

--- a/solution.py
+++ b/solution.py
@@ -116,43 +116,81 @@
     block = upper.shape[0]
     reduced = nt(nn(inverse, blocks([[m1, m2], [m2, m3]])), inverse)
     tilted = filtered(reduced, lambda square: nn(square[:, :block], upper))
-    return reduced, tilted, tn(tilted, tilted)
-
-
-def ritz_one(inverse, reduced, tilted, gram):
-    _, normal = cholesky_and_inverse(gram)
-    orthonormal = nt(tilted, normal)
-    coeffs = tn(inverse, orthonormal)
-    return coeffs, tn(orthonormal, nn(reduced, orthonormal))
-
-
-def basis_two(coeffs, theta, moments):
-    m0, m1, m2, m3, m4 = moments
-    block = theta.shape[0]
+    return tilted, tn(tilted, tilted)
+
+
+def hankel(moments):
+    return blocks([moments[i : i + 3] for i in range(3)])
+
+
+def diagonal(part, count):
+    zero = jnp.zeros_like(part)
+    return blocks([[part if i == j else zero for j in range(count)] for i in range(count)])
+
+
+def ritz_one(inverse, tilted, gram, moments, powers):
+    block = gram.shape[0]
+    coeffs = tn(inverse, tilted)
     head, tail = coeffs[:block], coeffs[block:]
     zero = jnp.zeros_like(head)
-    gram = blocks([[m0, m1, m2], [m1, m2, m3], [m2, m3, m4]])
-    current = jnp.concatenate([head, tail, zero], axis=0)
-    search = jnp.concatenate([zero, tail, zero], axis=0)
-    residual = jnp.concatenate([zero, head, tail], axis=0) - nn(current, theta)
-    gram_current = nn(gram, current)
-    search = search - nn(current, tn(gram_current, search))
-    gram_search = nn(gram, search)
-    _, normal = cholesky_and_inverse(tn(search, gram_search))
-    search = nt(search, normal)
-    gram_search = nt(gram_search, normal)
-    residual = residual - nn(search, tn(gram_search, residual))
-    _, normal = cholesky_and_inverse(tn(residual, nn(gram, residual)))
-    residual = nt(residual, normal)
-    basis = jnp.concatenate([current, search, residual], axis=1)
-    mixed = blocks([[m1, m2, m3], [m2, m3, m4], [m3, m4, zero]])
-    return basis, tn(basis, nn(mixed, basis))
-
-
-def ritz_kernel(scale, sums_ref, basis_ref, partial_ref, rotated_ref, eigen_ref, ritz_ref):
+    spanned = blocks([[zero, zero, head], [tail, head, tail], [zero, tail, zero]])
+    _, normal = cholesky_and_inverse(gram)
+    products = tn(spanned, nn(hankel(moments), spanned[:, : 2 * block]))
+    mixed = tn(spanned, nn(hankel(moments[1:] + [zero]), spanned))
+    rotated = tn(spanned, powers)
+    thrice = diagonal(normal, 3)
+    return (
+        nt(tail, normal),
+        nt(nn(thrice, products), diagonal(normal, 2)),
+        nt(nn(thrice, mixed), thrice),
+        nn(thrice, rotated),
+    )
+
+
+def residual_and_search(products):
+    block = products.shape[1] // 2
+    along = products[2 * block :]
+    return along, products[: 2 * block] - tn(along, along)
+
+
+def eliminate_search(along, left):
+    block = along.shape[0]
+    shared, theta = along[:, :block], along[:, block:]
+    _, normal = cholesky_and_inverse(left[:block, :block])
+    overlap = nn(normal, left[:block, block:])
+    return normal, overlap, left[block:, block:] - tn(overlap, overlap), shared, theta
+
+
+def basis_two(normal, overlap, rest, shared, theta, mixed, rotated):
+    block = rest.shape[0]
+    zero = jnp.zeros_like(rest)
+    _, last = cholesky_and_inverse(rest)
+    search = normal.T
+    along = nn(shared, search)
+    turn = blocks(
+        [
+            [zero, search, -nn(search, overlap)],
+            [zero, zero, eye(block)],
+            [eye(block), -along, nn(along, overlap) - theta],
+        ]
+    )
+    mixed = tn(turn, nn(mixed, turn))
+    rotated = tn(turn, rotated)
+    above, below = mixed[: 2 * block], nn(last, mixed[2 * block :])
+    reduced = blocks(
+        [
+            [above[:, : 2 * block], nt(above[:, 2 * block :], last)],
+            [below[:, : 2 * block], nt(below[:, 2 * block :], last)],
+        ]
+    )
+    rotated = jnp.concatenate([rotated[: 2 * block], nn(last, rotated[2 * block :])], axis=0)
+    return last, reduced, rotated
+
+
+def ritz_kernel(scale, sums_ref, tail_ref, partial_ref, rotated_ref, eigen_ref, ritz_ref):
     block = ritz_ref.shape[0]
     last = mean_with_transpose(sums_ref[:, :block] * scale)
-    tail = basis_ref[2 * block :, 2 * block :]
+    tail = tail_ref[...]
     zero = jnp.zeros((block, block), jnp.float32)
     corner = tn(tail, nn(last, tail))
     reduced = partial_ref[...] + blocks(
@@ -166,10 +204,6 @@
     ritz_ref[...] = nt(nn(normal, projected), normal)
 
 
-def each(low, high, body):
-    lax.fori_loop(low, high, lambda k, c: (body(k), c)[1], 0)
-
-
 def far_first(count):
     return sorted(range(1, count), key=lambda k: -min(k, count - k))
 
@@ -181,7 +215,7 @@
     links_ref,
     weight_ref,
     slot_ref,
-    basis_ref,
+    tail_ref,
     partial_ref,
     rotated_ref,
     last_ref,
@@ -260,42 +294,64 @@
     def greet(d, s):
         pl.semaphore_signal(barrier, inc=1, device_id=(d, s), device_id_type=MESH)
 
-    for k in far_first(n_sub):
-        greet(dom, sub_peer(k))
-    for k in range(n_sub):
-        greet(dom_peer(0), k)
-        greet(dom_peer(2), k)
     for k in far_first(N_Z):
         greet(row * N_Z + z_peer(k), sub)
     for k in far_first(n_y):
         greet(y_peer(k) * N_Z + col, sub)
-
-    def rs_copy(j, peer, at):
-        return remote(contrib.at[j, peer], gathered.at[j, at],
-                      rs_send.at[j, peer], rs_recv.at[j, at], dom, peer)
-
-    def ag_copy(j, to, peer, area, at):
-        return remote(pools.at[j, 1, sub], pools.at[j, area, at],
-                      ag_send.at[j, to, peer], ag_recv.at[j, area, at], dom_peer(to), peer)
+    for k in far_first(n_sub) + [0]:
+        greet(dom_peer(0), sub_peer(k))
+        greet(dom_peer(2), sub_peer(k))
+    for k in far_first(n_sub):
+        greet(dom, sub_peer(k))
+
+    def bulk(ref, send, recv):
+        return remote(ref, ref, send, recv, dom, sub_peer(1))
+
+    def rs_copy(j, peer):
+        return remote(contrib.at[j, peer], gathered.at[j, sub],
+                      rs_send.at[j], rs_recv.at[j], dom, peer)
+
+    def rs_all(j):
+        return bulk(gathered.at[j, 0 : n_sub - 1], rs_send.at[j], rs_recv.at[j])
+
+    def ag_copy(j, to, peer, area):
+        return remote(pools.at[j, 1, sub], pools.at[j, area, sub],
+                      ag_send.at[j, to], ag_recv.at[j, area], dom_peer(to), peer)
+
+    def ag_all(j, area):
+        some = pools.at[j, area, 0 : n_sub - 1] if area == 1 else pools.at[j, area]
+        return bulk(some, ag_send.at[j, area], ag_recv.at[j, area])
 
     def rows_of(p):
         return pl.ds(pl.multiple_of(p * share, share), share)
 
-    def part_copy(b, peer, at):
-        return remote(own[b].at[rows_of(peer)], part_in[b].at[at],
-                      part_send.at[b, peer], part_recv.at[b, at], dom, peer)
-
-    def z_copy(b, peer, at):
-        return remote(z_in[b].at[col], z_in[b].at[at],
-                      z_send.at[b, peer], z_recv.at[b, at], row * N_Z + peer, sub)
-
-    def y_copy(b, peer, at):
-        return remote(y_in[b].at[row], y_in[b].at[at],
-                      y_send.at[b, peer], y_recv.at[b, at], peer * N_Z + col, sub)
-
-    def out_copy(b, peer, at):
-        return remote(sums[b].at[rows_of(sub)], sums[b].at[rows_of(at)],
-                      out_send.at[b, peer], out_recv.at[b, at], dom, peer)
+    def part_copy(b, peer):
+        return remote(own[b].at[rows_of(peer)], part_in[b].at[sub],
+                      part_send.at[b], part_recv.at[b], dom, peer)
+
+    def part_all(b):
+        return bulk(part_in[b].at[0 : n_sub - 1], part_send.at[b], part_recv.at[b])
+
+    def z_copy(b, peer):
+        return remote(z_in[b].at[col], z_in[b].at[col],
+                      z_send.at[b], z_recv.at[b], row * N_Z + peer, sub)
+
+    def z_all(b):
+        return bulk(z_in[b].at[0 : N_Z - 1], z_send.at[b], z_recv.at[b])
+
+    def y_copy(b, peer):
+        return remote(y_in[b].at[row], y_in[b].at[row],
+                      y_send.at[b], y_recv.at[b], peer * N_Z + col, sub)
+
+    def y_all(b):
+        return bulk(y_in[b].at[0 : n_y - 1], y_send.at[b], y_recv.at[b])
+
+    def out_copy(b, peer):
+        return remote(sums[b].at[rows_of(sub)], sums[b].at[rows_of(sub)],
+                      out_send.at[b], out_recv.at[b], dom, peer)
+
+    def out_all(b):
+        return bulk(sums[b].at[0 : (n_sub - 1) * share], out_send.at[b], out_recv.at[b])
 
     def total(ref, count):
         result = ref[0]
@@ -305,47 +361,40 @@
 
     def sum_begin(b):
         for k in far_first(n_sub):
-            part_copy(b, sub_peer(k), sub).start()
+            part_copy(b, sub_peer(k)).start()
         part_in[b][sub] = own[b][rows_of(sub), :]
 
     def sum_along_z(b):
-        for k in far_first(n_sub)[::-1]:
-            part_copy(b, sub_peer(k), sub_peer(k)).wait_recv()
+        part_all(b).wait_recv()
         z_in[b][col] = total(part_in[b], n_sub)
         for k in far_first(N_Z):
-            z_copy(b, z_peer(k), col).start()
+            z_copy(b, z_peer(k)).start()
 
     def sum_along_y(b):
-        for k in far_first(N_Z)[::-1]:
-            z_copy(b, z_peer(k), z_peer(k)).wait_recv()
+        z_all(b).wait_recv()
         y_in[b][row] = total(z_in[b], N_Z)
         for k in far_first(n_y):
-            y_copy(b, y_peer(k), row).start()
+            y_copy(b, y_peer(k)).start()
 
     def sum_back(b):
-        for k in far_first(n_y)[::-1]:
-            y_copy(b, y_peer(k), y_peer(k)).wait_recv()
+        y_all(b).wait_recv()
         sums[b][rows_of(sub), :] = total(y_in[b], n_y)
         for k in far_first(n_sub):
-            out_copy(b, sub_peer(k), sub).start()
+            out_copy(b, sub_peer(k)).start()
 
     def sum_end(b):
-        for k in far_first(n_sub)[::-1]:
-            out_copy(b, sub_peer(k), sub_peer(k)).wait_recv()
+        out_all(b).wait_recv()
 
     def sum_sent(b):
-        each(1, n_sub, lambda k: part_copy(b, sub_peer(k), sub).wait_send())
-        each(1, N_Z, lambda k: z_copy(b, z_peer(k), col).wait_send())
-        each(1, n_y, lambda k: y_copy(b, y_peer(k), row).wait_send())
-        each(1, n_sub, lambda k: out_copy(b, sub_peer(k), sub).wait_send())
+        for copies in (part_all, z_all, y_all, out_all):
+            copies(b).wait_send()
 
     def rs_sent(j):
-        each(1, n_sub, lambda k: rs_copy(j, sub_peer(k), sub).wait_send())
+        rs_all(j).wait_send()
 
     def ag_sent(j):
-        each(1, n_sub, lambda k: ag_copy(j, 1, sub_peer(k), 1, sub).wait_send())
-        each(0, n_sub, lambda k: ag_copy(j, 0, k, 2, sub).wait_send())
-        each(0, n_sub, lambda k: ag_copy(j, 2, k, 0, sub).wait_send())
+        for area in range(3):
+            ag_all(j, area).wait_send()
 
     root_ref[...] = lax.rsqrt(jnp.sum(weight_ref[...], axis=0, keepdims=True))
 
@@ -399,25 +448,20 @@
         if j == 0:
             pl.semaphore_wait(barrier, 3 * n_sub - 1 + N_Z - 1 + n_y - 1)
         for k in far_first(n_sub):
-            rs_copy(j, sub_peer(k), sub).start()
+            rs_copy(j, sub_peer(k)).start()
         gathered[j, sub] = contrib[j, sub]
         while_reduced()
         summed = apply(high, low, 0, nodes)
-        for k in far_first(n_sub)[::-1]:
-            rs_copy(j, sub_peer(k), sub_peer(k)).wait_recv()
+        rs_all(j).wait_recv()
         pools[j, 1, sub] = total(gathered.at[j], n_sub)
         for k in far_first(n_sub) + [0]:
-            ag_copy(j, 0, sub_peer(k), 2, sub).start()
-            ag_copy(j, 2, sub_peer(k), 0, sub).start()
+            ag_copy(j, 0, sub_peer(k), 2).start()
+            ag_copy(j, 2, sub_peer(k), 0).start()
         for k in far_first(n_sub):
-            ag_copy(j, 1, sub_peer(k), 1, sub).start()
+            ag_copy(j, 1, sub_peer(k), 1).start()
         while_gathered()
-        for k in range(1, n_sub):
-            ag_copy(j, 1, sub_peer(k), 1, sub_peer(k)).wait_recv()
         for area in (1, 0, 2):
-            if area != 1:
-                for k in range(n_sub):
-                    ag_copy(j, area, k, area, k).wait_recv()
+            ag_all(j, area).wait_recv()
             high, low = split(pools[j, area].reshape(block, slots))
             summed = summed + apply(high, low, nodes + area * slots, slots)
         return summed
@@ -441,50 +485,50 @@
         sum_along_z(0)
         rs_sent(1)
 
-    def moments_third():
-        own_b[:, 0:block] = nt(one_ref[...], two_ref[...])
-        own_b[:, block:] = nt(two_ref[...], two_ref[...])
-        sum_begin(1)
+    def third_reduced():
         sum_along_y(0)
         ag_sent(1)
+        sum_along_z(1)
 
     def third_gathered():
         sum_back(0)
-        sum_along_z(1)
         rs_sent(2)
+        sum_along_y(1)
 
     one_ref[...] = affinity(0, start_ref[...], build_table, moments_first)
     two_ref[...] = affinity(1, one_ref[...], moments_second, second_gathered)
-    three = affinity(2, two_ref[...], moments_third, third_gathered)
+    own_b[:, 0:block] = nt(one_ref[...], two_ref[...])
+    own_b[:, block:] = nt(two_ref[...], two_ref[...])
+    sum_begin(1)
+    three = affinity(2, two_ref[...], third_reduced, third_gathered)
     own_c[:, 0:block] = nt(two_ref[...], three)
 
     def moment(b, c):
         return mean_with_transpose(sums[b][:, c * block : (c + 1) * block] * scale)
 
     sum_begin(2)
-    sum_along_y(1)
     sum_end(0)
     m0, m1, m2 = moment(0, 0), moment(0, 1), moment(0, 2)
     upper, first, below, rest = factor_one(m0, m1, m2)
+    sum_back(1)
     sum_along_z(2)
-    sum_back(1)
     inverse = inverse_one(first, below, rest)
-    ag_sent(2)
-    sum_sent(0)
     sum_end(1)
     m3, m4 = moment(1, 0), moment(1, 1)
-    reduced, tilted, gram = filter_one(inverse, upper, m1, m2, m3)
+    tilted, gram = filter_one(inverse, upper, m1, m2, m3)
     sum_along_y(2)
-    coeffs, theta = ritz_one(inverse, reduced, tilted, gram)
+    powers = jnp.concatenate([start_ref[...], one_ref[...], two_ref[...]], axis=0)
+    tail, products, mixed, rotated = ritz_one(inverse, tilted, gram, [m0, m1, m2, m3, m4], powers)
+    along, left = residual_and_search(products)
     sum_back(2)
-    basis, partial = basis_two(coeffs, theta, (m0, m1, m2, m3, m4))
-    basis_ref[...] = basis
+    normal, overlap, rest, shared, theta = eliminate_search(along, left)
+    last, partial, rotated = basis_two(normal, overlap, rest, shared, theta, mixed, rotated)
+    tail_ref[...] = nt(tail, last)
     partial_ref[...] = partial
-    rotated_ref[...] = tn(
-        basis, jnp.concatenate([start_ref[...], one_ref[...], two_ref[...]], axis=0)
-    )
-    sum_sent(1)
-    sum_sent(2)
+    rotated_ref[...] = rotated
+    ag_sent(2)
+    for b in range(len(WIDTHS)):
+        sum_sent(b)
     sum_end(2)
 
 
@@ -506,10 +550,10 @@
     def buffers(*shape):
         return [VMEM(shape + (width,), f32) for width in WIDTHS]
 
-    basis, partial, rotated, last = pl.pallas_call(
+    tail, partial, rotated, last = pl.pallas_call(
         functools.partial(sums_kernel, n_dom, n_sub),
         out_shape=(
-            array(3 * block, 3 * block),
+            array(block, block),
             array(3 * block, 3 * block),
             array(3 * block, nodes),
             array(block, WIDTHS[2]),
@@ -531,11 +575,11 @@
             *buffers(N_Z, share),
             *buffers(n_y, share),
             *buffers(block)[:2],
-            DMA((ROUNDS, n_sub)),
-            DMA((ROUNDS, n_sub)),
-            DMA((ROUNDS, 3, n_sub)),
-            DMA((ROUNDS, 3, n_sub)),
-            *[DMA((len(WIDTHS), size)) for size in (n_sub, N_Z, n_y, n_sub) for _ in range(2)],
+            DMA((ROUNDS,)),
+            DMA((ROUNDS,)),
+            DMA((ROUNDS, 3)),
+            DMA((ROUNDS, 3)),
+            *[DMA((len(WIDTHS),)) for _ in range(8)],
         ],
         compiler_params=pltpu.CompilerParams(
             collective_id=0, has_side_effects=True, vmem_limit_bytes=limit
@@ -549,7 +593,7 @@
         out_specs=(vmem,) * 2,
         compiler_params=pltpu.CompilerParams(vmem_limit_bytes=limit),
         name="ritz_steps",
-    )(last, basis, partial, rotated)
+    )(last, tail, partial, rotated)
 
 
 def solution(mesh):

time: 96.3 us -> 89.2 us (0.926)
  Pallas kernels: 92.3 us -> 85.3 us
    pallas_call x1, Pallas kernels: 87.7 us -> 80.6 us  [per_device(): pl.pallas_call(functools.partial(sums_kernel, n_dom, n_sub), out_shape=(a...]
where the time goes in v4:
time: 89.2 us; the launch traced here: 88.9 us
  Pallas kernels  85.3 us (96%)
  local copies, waits for them, and re-layouts  2.98 us (3%)
    pallas_call x1, Pallas kernels, per_device(): pl.pallas_call(functools.partial(sums_kernel, n_dom, n_sub), out_shape=(a...  80.6 us
    pallas_call x1, Pallas kernels, per_device(): pl.pallas_call(functools.partial(ritz_kernel, 1.0 / (nodes * n_dom * n_su...  4.63 us
    unnamed x8, local copies, waits for them, and re-layouts  2.98 us

profile of v4, /device:TPU:1, one launch (start us, length us, event | category | flops | bytes accessed | tf_op | source)
XLA Modules:
  0.0 88.9 jit_solution(10967105749663625112)
XLA Ops:
  0.6 0.0 copy-start.3
  0.6 0.7 copy-done.3
  1.3 0.0 copy-start
  1.3 0.8 copy-done
  2.2 0.0 copy-start.1
  2.2 0.7 copy-done.1
  2.9 0.0 copy-start.2
  2.9 0.7 copy-done.2
  3.6 80.6 %powers_and_sums.1 = (f32[64,64]{1,0:T(8,128)S(1)}, f32[192,192]{1,0:T(8,128)S(1)}, f32[192,256]{1,0:T(8,128)S(1)}, f32[64,128]{1,0:T(8,128)S(1)}) custom-call(f32[64,256]{1,0:T(8,128)S(1)} %copy-done, s32[20,256]{1,0:T(8,128)S(1)} %copy-done.1, f32[20,256]{1,0:T(8,128)S(1)} %copy-done.2, s32[1,256]{1,0:T(1,128)S(1)} %bitcast.1), custom_call_target="tpu_custom_call" | custom-call | tf_op jit(solution)/shard_map/powers_and_sums/pallas_call | solution.py:553
  84.3 4.6 %ritz_steps.1 = (f32[64,256]{1,0:T(8,128)}, f32[64,64]{1,0:T(8,128)}) custom-call(f32[64,128]{1,0:T(8,128)S(1)} %get-tuple-element.6.sums_ref, f32[64,64]{1,0:T(8,128)S(1)} %get-tuple-element.7.tail_ref, f32[192,192]{1,0:T(8,128)S(1)} %get-tuple-element.8.partial_ref, f32[192,256]{1,0:T(8,128)S(1)} %get-tuple-element.9.rotated_ref), custom_call_target="tpu_custom_call" | custom-call | tf_op jit(solution)/shard_map/ritz_steps/pallas_call | solution.py:589
Async XLA Ops:
  0.6 0.7 copy-start.3
  1.3 0.8 copy-start
  2.2 0.7 copy-start.1
  2.9 0.7 copy-start.2

commit v5 on v4

--- a/solution.py
+++ b/solution.py
@@ -466,10 +466,14 @@
             summed = summed + apply(high, low, nodes + area * slots, slots)
         return summed
 
+    parts = table_hi.shape[0] // BUILD_ROWS
+    early = (nodes + slots) // BUILD_ROWS
+
     def build_table():
-        lax.fori_loop(0, table_hi.shape[0] // BUILD_ROWS, build, 0)
+        lax.fori_loop(0, early, build, 0)
 
     def moments_first():
+        lax.fori_loop(early, parts, build, 0)
         own_a[:, 0:block] = nt(start_ref[...], start_ref[...])
         own_a[:, 3 * block :] = jnp.zeros((block, block), jnp.float32)
         own_c[:, block:] = jnp.zeros((block, block), jnp.float32)

time: 89.2 us -> 89.4 us (level)
  no operation moved by 1% of the time
where the time goes in v5:
time: 89.4 us; the launch traced here: 89 us
  Pallas kernels  85.4 us (96%)
  local copies, waits for them, and re-layouts  2.98 us (3%)
    pallas_call x1, Pallas kernels, per_device(): pl.pallas_call(functools.partial(sums_kernel, n_dom, n_sub), out_shape=(a...  80.8 us
    pallas_call x1, Pallas kernels, per_device(): pl.pallas_call(functools.partial(ritz_kernel, 1.0 / (nodes * n_dom * n_su...  4.63 us
    unnamed x8, local copies, waits for them, and re-layouts  2.98 us

profile of v5, /device:TPU:1, one launch (start us, length us, event | category | flops | bytes accessed | tf_op | source)
XLA Modules:
  0.0 89.0 jit_solution(7844812102894802473)
XLA Ops:
  0.6 0.0 copy-start.3
  0.6 0.7 copy-done.3
  1.3 0.0 copy-start
  1.3 0.8 copy-done
  2.2 0.0 copy-start.1
  2.2 0.7 copy-done.1
  2.9 0.0 copy-start.2
  2.9 0.7 copy-done.2
  3.6 80.8 %powers_and_sums.1 = (f32[64,64]{1,0:T(8,128)S(1)}, f32[192,192]{1,0:T(8,128)S(1)}, f32[192,256]{1,0:T(8,128)S(1)}, f32[64,128]{1,0:T(8,128)S(1)}) custom-call(f32[64,256]{1,0:T(8,128)S(1)} %copy-done, s32[20,256]{1,0:T(8,128)S(1)} %copy-done.1, f32[20,256]{1,0:T(8,128)S(1)} %copy-done.2, s32[1,256]{1,0:T(1,128)S(1)} %bitcast.1), custom_call_target="tpu_custom_call" | custom-call | tf_op jit(solution)/shard_map/powers_and_sums/pallas_call | solution.py:557
  84.4 4.6 %ritz_steps.1 = (f32[64,256]{1,0:T(8,128)}, f32[64,64]{1,0:T(8,128)}) custom-call(f32[64,128]{1,0:T(8,128)S(1)} %get-tuple-element.6.sums_ref, f32[64,64]{1,0:T(8,128)S(1)} %get-tuple-element.7.tail_ref, f32[192,192]{1,0:T(8,128)S(1)} %get-tuple-element.8.partial_ref, f32[192,256]{1,0:T(8,128)S(1)} %get-tuple-element.9.rotated_ref), custom_call_target="tpu_custom_call" | custom-call | tf_op jit(solution)/shard_map/ritz_steps/pallas_call | solution.py:593
Async XLA Ops:
  0.6 0.7 copy-start.3
  1.3 0.8 copy-start
  2.2 0.7 copy-start.1
  2.9 0.7 copy-start.2
